TPU v7x, 256 devices: a whole 4x4x8 slice. The times are simulated.
256 devices in a mesh: stream: 64 (over z_hi, y, x), girth: 4 (over z_lo, core).
Axes of the slice: x: 4, y: 4, z: 8 (z_hi: 4, z_lo: 2; z = z_hi * 2 + z_lo), core: 2. Of those that a mesh axis runs over, the one named last changes fastest.
Arguments:
- eta_hat: float32 [4096, 4096], P('stream', 'girth'), may hold values from -0.0014648438 to 0.0014648438
- phi_hat: float32 [4096, 4096], P('stream', 'girth'), may hold values from -0.0014648438 to 0.0014648438
- zone_rows: int32 [64, 8], replicated, may hold values from 0 to 4095
- zone_count: int32 [64], P('stream'), may hold values from 1 to 8, as said below
- volume: float32 [512, 48, 4096], P('stream', None, 'girth'), may hold values from 0 to 1
- lift: float32 [512, 48, 4096], P('stream', None, 'girth'), may hold values from -3 to 3
- stream_speed: float32 [512, 48, 4096], P('stream', None, 'girth'), may hold values from 0.5 to 1.5
- surface_blocks: int32 [512, 6], P('stream'), may hold values 0 or 1
Outputs:
- volume_next: float32 [512, 48, 4096], P('stream', None, 'girth')
- lift_next: float32 [512, 48, 4096], P('stream', None, 'girth')
Inputs may be any that keep to these rules, and one draw needn't show every extreme that they name: `zone_count`: each slab has 1 to 8 zone planes and some slab has exactly 8.
All inputs are finite; a program needn't handle non-finite values. No bound on the sum of `surface_blocks` on one device may be relied on, other than what follows from the above.
Results may differ from a plain program's by a relative error of at most 0.00017.
Values sent between devices are 32-bit elements; how exact they have to be, the bound alone decides.
A program may use at most 128 MiB of HBM per device.

v0:
```python
import math

import jax
import jax.numpy as jnp
from jax import lax
from jax.sharding import PartitionSpec as P

depth_scale = 2.0
cell_height = 0.125


def padded_2(value, sides, width):
    for axis, dim in sides:
        devices, length = (lax.axis_size(axis), value.shape[dim])
        up = [(i, (i + 1) % devices) for i in range(devices - 1)]
        down = [(j, i) for i, j in up]
        last = lax.slice_in_dim(value, length - width, length, axis=dim)
        initial = lax.slice_in_dim(value, 0, width, axis=dim)
        before = lax.ppermute(last, axis, up)
        after = lax.ppermute(initial, axis, down)
        value = jnp.concatenate([before, value, after], axis=dim)
    return value


def signed_freq(mode_idx, extent):
    half_size = extent // 2
    shifted = jnp.where(mode_idx < half_size, mode_idx, mode_idx - extent)
    return 2.0 * shifted.astype(jnp.float32) / extent


def cas_pair(left_ids, right_ids, extent):
    phases = (left_ids[:, None] * right_ids[None, :] % extent).astype(jnp.float32) * (
        2.0 * math.pi / extent
    )
    return (jnp.cos(phases) + jnp.sin(phases), jnp.cos(phases) - jnp.sin(phases))


def product(left_mat, right_mat):
    return jnp.dot(left_mat, right_mat, precision=lax.Precision.HIGHEST)


def relax(fraction, lift_now, height, rise_rate, zone_count):
    zone_span = fraction.shape[1]
    layers = fraction.shape[2]
    levels = (jnp.arange(layers, dtype=jnp.float32) - layers / 2 + 0.5) * cell_height
    gap_up = levels[None, None, :, None] - height[:, :, None, :]
    fraction_goal = jnp.clip(0.5 - gap_up / cell_height, 0.0, 1.0)
    lift_goal = rise_rate[:, :, None, :] * jnp.exp(0.5 * jnp.minimum(gap_up, 0.0))
    plane_idx = jnp.arange(zone_span, dtype=jnp.float32)[None, :]
    totals = zone_count.astype(jnp.float32)[:, None]
    stretch = jnp.minimum((plane_idx + 0.5) / totals, 1.0)
    weights = jnp.where(
        plane_idx < totals, 1.0 - (jnp.exp(stretch**3.5) - 1.0) / (math.e - 1.0), 0.0
    )
    weights = weights[:, :, None, None]
    return (
        weights * fraction_goal + (1.0 - weights) * fraction,
        weights * lift_goal + (1.0 - weights) * lift_now,
    )


def advance(flux_x, volume_pad, lift_pad, surface_marks):
    fraction = volume_pad[1:-1, :, 1:-1]
    lift_now = lift_pad[1:-1, :, 1:-1]
    upwind = flux_x[1:-1, :, 1:-1] - flux_x[:-2, :, 1:-1]
    spread = volume_pad[1:-1, :, 2:] + volume_pad[1:-1, :, :-2] - 2.0 * fraction
    vertical = (
        jnp.maximum(lift_now[:, :-1], 0.0) * fraction[:, :-1]
        + jnp.minimum(lift_now[:, :-1], 0.0) * fraction[:, 1:]
    )
    boundary = jnp.zeros_like(fraction[:, :1])
    face_flux = jnp.concatenate([boundary, vertical, boundary], axis=1)
    divergence = face_flux[:, 1:] - face_flux[:, :-1]
    sharpen = surface_marks * fraction * (1.0 - fraction) * (2.0 * fraction - 1.0)
    volume_next = fraction - 0.3 * upwind - 0.3 * divergence + 0.1 * spread + 2.0 * sharpen
    padded_z = jnp.pad(lift_now, ((0, 0), (1, 1), (0, 0)))
    beside_all = (
        lift_pad[2:, :, 1:-1]
        + lift_pad[:-2, :, 1:-1]
        + lift_pad[1:-1, :, 2:]
        + lift_pad[1:-1, :, :-2]
    )
    beside_all = beside_all + padded_z[:, 2:] + padded_z[:, :-2]
    lift_next = lift_now + 0.15 * (beside_all - 6.0 * lift_now)
    return (volume_next, lift_next)


def on_device(eta_hat, phi_hat, zone_rows, zone_count, volume, lift, stream_speed, surface_blocks):
    rows_here, cols_here = eta_hat.shape
    stripes = lax.axis_size("stream")
    nx_all = rows_here * stripes
    ny_all = cols_here * lax.axis_size("girth")
    kx_here = lax.axis_index("stream") * rows_here + jnp.arange(rows_here, dtype=jnp.int32)
    ky_here = lax.axis_index("girth") * cols_here + jnp.arange(cols_here, dtype=jnp.int32)
    freq_x = signed_freq(kx_here, nx_all)
    freq_y = signed_freq(ky_here, ny_all)
    wavenum = jnp.sqrt(freq_x[:, None] ** 2 + freq_y[None, :] ** 2)
    lift_hat = wavenum * jnp.tanh(depth_scale * wavenum) * phi_hat
    pieces = (
        lax.all_gather(eta_hat, "girth", axis=1, tiled=True),
        lax.all_gather(lift_hat, "girth", axis=1, tiled=True),
    )
    mode_count = pieces[0].shape[1]
    mode_ids = jnp.arange(mode_count, dtype=jnp.int32)
    even_tab, odd_tab = cas_pair(mode_ids, ky_here, ny_all)
    slope_tab = signed_freq(mode_ids, ny_all)[:, None] * odd_tab
    y_done = product(pieces[0], even_tab)
    y_slope = product(pieces[0], slope_tab)
    y_lift = product(pieces[1], even_tab)
    zone_span = zone_rows.shape[1]
    zone_list = zone_rows.reshape(-1)
    even_x, odd_x = cas_pair(zone_list, kx_here, nx_all)
    slope_x = odd_x * freq_x[None, :]
    partial_value = jnp.stack(
        [
            product(even_x, y_done),
            product(slope_x, y_done),
            product(even_x, y_slope),
            product(even_x, y_lift),
        ]
    )
    partial_value = partial_value.reshape(4, stripes, zone_span, cols_here)
    summed = jnp.sum(
        lax.all_to_all(partial_value, "stream", split_axis=1, concat_axis=1, tiled=True), axis=1
    )
    height = summed[0]
    rise_rate = (1.0 + summed[1] * summed[1] + summed[2] * summed[2]) * summed[3]
    head_volume, head_lift = relax(
        volume[None, :zone_span], lift[None, :zone_span], height[None], rise_rate[None], zone_count
    )
    relaxed_volume = jnp.concatenate([head_volume[0], volume[zone_span:]], axis=0)
    relaxed_lift = jnp.concatenate([head_lift[0], lift[zone_span:]], axis=0)
    flux_field = stream_speed * relaxed_volume
    surface_marks = jnp.repeat(surface_blocks, 8, axis=1)[:, :, None].astype(jnp.float32)
    stacked = jnp.stack([flux_field, relaxed_volume, relaxed_lift])
    padded = padded_2(stacked, (("stream", 1), ("girth", 3)), 1)
    return advance(padded[0], padded[1], padded[2], surface_marks)


def solution(mesh):
    return jax.shard_map(
        on_device,
        mesh=mesh,
        in_specs=(
            P("stream", "girth"),
            P("stream", "girth"),
            P(),
            P("stream"),
            P("stream", None, "girth"),
            P("stream", None, "girth"),
            P("stream", None, "girth"),
            P("stream", None),
        ),
        out_specs=(P("stream", None, "girth"), P("stream", None, "girth")),
        check_vma=False,
    )
```

profile of v0, /device:TPU:31, one launch (start us, length us, event | category | flops | bytes accessed | tf_op | source)
XLA Modules:
  0.0 581.4 jit_solution(5396931785503180696)
XLA Ops:
  10.8 26.0 %all-gather.5.cloned.1.call-done = f32[64,4096]{1,0:T(8,128)} async-done(((f32[64,1024]{1,0:T(8,128)}), f32[64,4096]{1,0:T(8,128)}) %all-gather.5.cloned.1.call-update) | async-done | bytes 1048592 | tf_op jit(solution)/shard_map/all_gather | solution.py:101
  36.8 79.2 %fusion.15 = f32[64,1024]{1,0:T(8,128)S(1)} fusion(f32[64,4096]{1,0:T(8,128)} %all-gather.5.cloned.1.call-done, s32[1024]{0:T(1024)S(1)} %iota_add_fusion), kind=kOutput, calls=%fused_computation.17 | convolution fusion | flops 3284140032 | bytes 1314816 | tf_op jit(solution)/shard_map/dot_general | solution.py:39
  116.0 2.8 convolution_bitcast_fusion
  118.9 89.8 %fusion.17 = f32[1024,64]{0,1:T(8,128)S(1)} fusion(f32[64,4096]{1,0:T(8,128)} %all-gather.3.cloned.1.call-done, s32[1024]{0:T(1024)S(1)} %iota_add_fusion), kind=kOutput, calls=%fused_computation.18 | convolution fusion | flops 3284140032 | bytes 1314816 | tf_op jit(solution)/shard_map/dot_general | solution.py:39
  208.7 2.8 convolution_bitcast_fusion.3
  211.5 2.8 convolution_bitcast_fusion.2
  214.4 79.3 %fusion.3 = f32[1024,64]{0,1:T(8,128)S(1)} fusion(f32[64,4096]{1,0:T(8,128)S(1)} %copy-done.4, f32[4096]{0:T(1024)S(1)} %fusion.61, s32[1024]{0:T(1024)S(1)} %iota_add_fusion), kind=kOutput, calls=%fused_computation.6 | convolution fusion | flops 3288334336 | bytes 1331200 | tf_op jit(solution)/shard_map/dot_general | solution.py:39
  293.6 2.8 convolution_bitcast_fusion.1
  296.4 3.6 pad_maximum_fusion
  300.0 11.9 %all-to-all-start = ((f32[4,64,8,1024]{3,2,0,1:T(8,128)}), f32[4,64,8,1024]{3,2,0,1:T(8,128)}, u32[]{:S(2)}, u32[]{:S(2)}) async-start(f32[4,64,8,1024]{3,2,0,1:T(8,128)} %pad_maximum_fusion), calls=%async_computation | async-start | bytes 16777216 | tf_op jit(solution)/shard_map/all_to_all | solution.py:124
  312.6 183.9 %all-to-all-done = f32[4,64,8,1024]{3,2,0,1:T(8,128)} async-done(((f32[4,64,8,1024]{3,2,0,1:T(8,128)}), f32[4,64,8,1024]{3,2,0,1:T(8,128)}, u32[]{:S(2)}, u32[]{:S(2)}) %all-to-all-start) | async-done | bytes 8388640 | tf_op jit(solution)/shard_map/all_to_all | solution.py:124
  496.5 3.9 reduce_sum.9
  500.4 2.3 multiply_bitcast_fusion
  504.7 3.4 collective-permute-start.1
  508.1 9.9 %collective-permute-done = f32[3,1,48,1024]{3,2,1,0:T(8,128)S(1)} collective-permute-done((f32[3,1,48,1024]{3,2,1,0:T(8,128)S(1)}, f32[3,1,48,1024]{3,2,1,0:T(8,128)S(1)}, u32[]{:S(2)}, u32[]{:S(2)}) %collective-permute-start) | collective-permute-done | bytes 589856 | tf_op jit(solution)/shard_map/ppermute | solution.py:19
  518.0 7.0 %collective-permute-done.1 = f32[3,1,48,1024]{3,2,1,0:T(8,128)S(1)} collective-permute-done((f32[3,1,48,1024]{3,2,1,0:T(8,128)S(1)}, f32[3,1,48,1024]{3,2,1,0:T(8,128)S(1)}, u32[]{:S(2)}, u32[]{:S(2)}) %collective-permute-start.1) | collective-permute-done | bytes 589856 | tf_op jit(solution)/shard_map/ppermute | solution.py:20
  525.8 2.5 copy-done
  528.8 20.3 %collective-permute-start.2 = (f32[3,10,48,1]{2,3,1,0:T(1,128)S(1)}, f32[3,10,48,1]{2,3,1,0:T(1,128)S(1)}, u32[]{:S(2)}, u32[]{:S(2)}) collective-permute-start(f32[3,10,48,1]{2,3,1,0:T(1,128)S(1)} %copy.30), channel_id=1, source_target_pairs={{0,1},{1,2},{2,3},{4,5},{5,6},{6,7},{8,9},{9,10},{10,11},{12,13},{... | collective-permute-start | bytes 17288 | tf_op jit(solution)/shard_map/ppermute | solution.py:19
  549.5 1.9 collective-permute-start.3
  551.9 2.6 collective-permute-done.3
  554.8 8.8 %concatenate.15 = f32[3,10,48,1026]{3,2,1,0:T(8,128)} concatenate(f32[3,10,48,1]{3,2,1,0:T(8,128)S(1)} %copy.28, f32[3,10,48,1024]{3,2,1,0:T(8,128)} %copy-done, f32[3,10,48,1]{3,2,1,0:T(8,128)S(1)} %copy.29), dimensions={3} | concatenate | bytes 11819520 | tf_op jit(solution)/shard_map/concatenate | solution.py:21
  563.6 3.4 slice_bitcast_fusion
  567.5 2.4 fusion.23
  571.2 2.9 fusion.37
  (40 shorter events, 9.7 us)
Async XLA Ops:
  7.2 29.6 %all-gather.5.cloned.1.call-start = ((), (), s32[]{:S(2)}) async-start(), calls=%async_computation.2 | async-start | bytes 1310720 | tf_op jit(solution)/shard_map/all_gather | solution.py:101
  9.1 109.8 %all-gather.3.cloned.1.call-start = ((), (), s32[]{:S(2)}) async-start(), calls=%async_computation.1 | async-start | bytes 1310720 | tf_op jit(solution)/shard_map/all_gather | solution.py:100
  208.7 5.6 copy-start.4
  300.0 196.5 %all-to-all-start = ((f32[4,64,8,1024]{3,2,0,1:T(8,128)}), f32[4,64,8,1024]{3,2,0,1:T(8,128)}, u32[]{:S(2)}, u32[]{:S(2)}) async-start(f32[4,64,8,1024]{3,2,0,1:T(8,128)} %pad_maximum_fusion), calls=%async_computation | async-start | bytes 16777216 | tf_op jit(solution)/shard_map/all_to_all | solution.py:124
  312.6 187.8 %copy-start.1 = (f32[8,48,1024]{2,1,0:T(8,128)S(1)}, f32[8,48,1024]{2,1,0:T(8,128)}, u32[]{:S(2)}) copy-start(f32[8,48,1024]{2,1,0:T(8,128)} %param.14) | copy-start | bytes 4718596
  312.6 187.8 %copy-start.2 = (f32[8,48,1024]{2,1,0:T(8,128)S(1)}, f32[8,48,1024]{2,1,0:T(8,128)}, u32[]{:S(2)}) copy-start(f32[8,48,1024]{2,1,0:T(8,128)} %param.12) | copy-start | bytes 4718596
  502.8 15.2 %collective-permute-start = (f32[3,1,48,1024]{3,2,1,0:T(8,128)S(1)}, f32[3,1,48,1024]{3,2,1,0:T(8,128)S(1)}, u32[]{:S(2)}, u32[]{:S(2)}) collective-permute-start(f32[3,1,48,1024]{3,2,1,0:T(8,128)S(1)} %get-tuple-element.9), channel_id=1, source_target_pairs={{0,4},{4,8},{8,12},{12,16},{16,20},{20,24},{24,28},{28,32},{32,36}... | collective-permute-start | bytes 1769480 | tf_op jit(solution)/shard_map/ppermute | solution.py:19
  504.7 20.3 %collective-permute-start.1 = (f32[3,1,48,1024]{3,2,1,0:T(8,128)S(1)}, f32[3,1,48,1024]{3,2,1,0:T(8,128)S(1)}, u32[]{:S(2)}, u32[]{:S(2)}) collective-permute-start(f32[3,1,48,1024]{3,2,1,0:T(8,128)S(1)} %get-tuple-element.10), channel_id=1, source_target_pairs={{4,0},{8,4},{12,8},{16,12},{20,16},{24,20},{28,24},{32,28},{36,32}... | collective-permute-start | bytes 1769480 | tf_op jit(solution)/shard_map/ppermute | solution.py:20
  525.8 2.5 copy-start
  528.3 23.1 %copy-start.3 = (s32[8,6]{1,0:T(8,128)S(1)}, s32[8,6]{1,0:T(8,128)}, u32[]{:S(2)}) copy-start(s32[8,6]{1,0:T(8,128)} %param.15) | copy-start | bytes 580
  528.8 22.7 %collective-permute-start.2 = (f32[3,10,48,1]{2,3,1,0:T(1,128)S(1)}, f32[3,10,48,1]{2,3,1,0:T(1,128)S(1)}, u32[]{:S(2)}, u32[]{:S(2)}) collective-permute-start(f32[3,10,48,1]{2,3,1,0:T(1,128)S(1)} %copy.30), channel_id=1, source_target_pairs={{0,1},{1,2},{2,3},{4,5},{5,6},{6,7},{8,9},{9,10},{10,11},{12,13},{... | collective-permute-start | bytes 17288 | tf_op jit(solution)/shard_map/ppermute | solution.py:19
  549.5 5.1 collective-permute-start.3
Sparse Core Ops, SparseCore 0:
  10.4 26.3 all-gather.4
  38.6 24.0 all-gather.2
where the time goes:
time: 590 us; the launch traced here: 581 us
  matrix products  260 us (44%)
  waiting for transfers between devices  230 us (39%)
  starting transfers between devices  39.5 us (7%)
  other arithmetic  19.1 us (3%)
  local copies, waits for them, and re-layouts  17.6 us (3%)
  between operations  15.4 us (3%)
    dot_general x7, matrix products, product(): return jnp.dot(left_mat, right_mat, precision=lax.Precision.HIGHEST)  260 us
    all_to_all x1, waiting for transfers between devices, on_device(): lax.all_to_all(partial_value, 'stream', split_axis=1, concat_axis=1, tile...  184 us
    all_gather x1, waiting for transfers between devices, on_device(): lax.all_gather(lift_hat, 'girth', axis=1, tiled=True)  26 us
    ppermute x2, starting transfers between devices, padded_2(): before = lax.ppermute(last, axis, up)  22.3 us
    all_to_all x1, starting transfers between devices, on_device(): lax.all_to_all(partial_value, 'stream', split_axis=1, concat_axis=1, tile...  11.9 us
  transfers between devices with their start and end apart: 7, of which 5 were waited for; matrix products, arithmetic and copies ran while one was open for 14% of the time, Pallas kernels for 0%

commit v1 on v0

v1 whole, which is shorter than its diff:
```python
import math

import jax
import jax.numpy as jnp
from jax import lax
from jax.experimental import pallas as pl
from jax.experimental.pallas import tpu as pltpu
from jax.sharding import PartitionSpec as P

F32 = jnp.float32
BF16 = jnp.bfloat16
MESH = pl.DeviceIdType.MESH
EXT = 1280

AG, RS, RZ, GA, HP, HN, RAW = 0, 12, 24, 30, 33, 37, 41
N_SEM = 49


def iota(shape, dim):
    return lax.broadcasted_iota(jnp.int32, shape, dim)


def quarter_turns(t):
    k = jnp.floor(t + 0.5)
    r = t - k
    r2 = r * r
    s = r * (
        1.5707963267949
        + r2 * (-0.645964097506 + r2 * (0.0796926262462 + r2 * (-0.00468175413532 + r2 * 0.000160441184787)))
    )
    c = 1.0 + r2 * (
        -1.23370055013617
        + r2 * (0.253669507901 + r2 * (-0.0208634807634 + r2 * (0.000919260274839 - r2 * 2.52020423731e-5)))
    )
    half = jnp.floor(k * 0.5)
    odd = (k - 2.0 * half) > 0.5
    sign = 1.0 - 2.0 * (half - 2.0 * jnp.floor(half * 0.5))
    return sign, odd, c, s


def cas_dcas(t):
    sign, odd, c, s = quarter_turns(t)
    plus, minus = c + s, c - s
    return sign * jnp.where(odd, minus, plus), sign * jnp.where(odd, -plus, minus)


def cos_sin(t):
    sign, odd, c, s = quarter_turns(t)
    return sign * jnp.where(odd, -s, c), sign * jnp.where(odd, c, s)


def split(value):
    hi = value.astype(BF16)
    return hi, (value - hi.astype(F32)).astype(BF16)


def dot(left, right):
    return jnp.dot(left, right, preferred_element_type=F32)


def dot3(left, right):
    (lh, ll), (rh, rl) = left, right
    return dot(lh, rh) + (dot(lh, rl) + dot(ll, rh))


def pick(index, values):
    out = values[-1]
    for i in range(len(values) - 2, -1, -1):
        out = jnp.where(index == i, values[i], out)
    return out


def wave_kernel(
    zr_ref, zc_ref, eta, phi, vol, lft, spd,
    hr, planes, cols,
    ag, tab, ps, ob, nb, zs, zo, zn, xg, xp, hmsg, hp, hn, e_hi, e_lo, perm, lhs, uu, hh,
    ssem, rsem,
):
    s = lax.axis_index("stream")
    g = lax.axis_index("girth")
    zh, y, x = s // 16, (s // 4) % 4, s % 4

    def at(zh_, y_, x_):
        return (zh_ * 16 + y_ * 4 + x_, g)

    def turn(c, d):
        return lax.rem(c + d + 4, 4)

    def on_x(d):
        return at(zh, y, turn(x, d))

    def on_y(d):
        return at(zh, turn(y, d), x)

    def on_z(d):
        return at(turn(zh, d), y, x)

    s_next = lax.rem(s + 1, 64)
    s_prev = lax.rem(s + 63, 64)

    def girth(j):
        return lax.rem(g + j, 4)

    targets = [on_x(1), on_x(-1), on_y(1), on_y(-1), on_z(1), on_z(-1)]
    targets += [(s, girth(j)) for j in (1, 2, 3)]
    targets += [(s_next, girth(j)) for j in range(4)]
    targets += [(s_prev, girth(j)) for j in range(4)]
    barrier = pltpu.get_barrier_semaphore()
    for device in targets:
        pl.semaphore_signal(barrier, inc=1, device_id=device, device_id_type=MESH)
    pl.semaphore_wait(barrier, len(targets))

    def copy(src, dst, index, device):
        return pltpu.make_async_remote_copy(
            src_ref=src, dst_ref=dst, send_sem=ssem.at[index], recv_sem=rsem.at[index],
            device_id=device, device_id_type=MESH,
        )

    sent = []

    def start(src, dst, index, device):
        c = copy(src, dst, index, device)
        c.start()
        sent.append(c)
        return c

    first = (on_x, on_y)
    second = (on_y, on_x)

    gat = {}
    for q in range(2):
        cs = pl.ds(q * 512, 512)
        ag[q, 0, 0] = eta[:, cs]
        gat[q, 0] = start(ag.at[q, 0, 0], ag.at[q, 0, 1], AG + 6 * q, first[q](1))
        gat[q, 1] = start(ag.at[q, 0, 0], ag.at[q, 0, 2], AG + 6 * q + 1, first[q](-1))
    kx_own = (s * 64 + iota((64, 1), 0)).astype(F32)
    fx_own = kx_own / 2048.0 - jnp.where(kx_own >= 2048.0, 2.0, 0.0)
    for q in range(2):
        cs = pl.ds(q * 512, 512)
        ky = (g * 1024 + q * 512 + iota((1, 512), 1)).astype(F32)
        fy = ky / 2048.0 - jnp.where(ky >= 2048.0, 2.0, 0.0)
        rad = jnp.sqrt(fx_own * fx_own + fy * fy)
        ag[q, 1, 0] = rad * jnp.tanh(2.0 * rad) * phi[:, cs]
        gat[q, 2] = start(ag.at[q, 1, 0], ag.at[q, 1, 1], AG + 6 * q + 2, first[q](1))
        gat[q, 3] = start(ag.at[q, 1, 0], ag.at[q, 1, 2], AG + 6 * q + 3, first[q](-1))

    raw = []
    edge_left, edge_right = pl.ds(0, 128), pl.ds(896, 128)
    to_right, to_left = (s, girth(1)), (s, girth(3))
    raw.append(start(vol.at[:, :, edge_right], cols.at[0], RAW, to_right))
    raw.append(start(lft.at[:, :, edge_right], cols.at[1], RAW + 1, to_right))
    raw.append(start(vol.at[:, :, edge_left], cols.at[2], RAW + 2, to_left))
    raw.append(start(lft.at[:, :, edge_left], cols.at[3], RAW + 3, to_left))

    zr = zr_ref[...].astype(F32)
    lane64 = iota((8, 64), 1)
    lane256 = iota((1, 256), 1)
    slot = lane256 // 64
    rel = (0, 1, -1, 2)
    for q in range(2):
        here = x if q == 0 else y
        coords = [turn(here, d) for d in (0, -1, 1, 2)]
        if q == 0:
            slabs = [zh * 16 + y * 4 + c for c in coords]
        else:
            slabs = [zh * 16 + c * 4 + x for c in coords]
        kx = (pick(slot, slabs) * 64 + lane256 % 64).astype(F32)
        fx = kx / 2048.0 - jnp.where(kx >= 2048.0, 2.0, 0.0)
        for r in range(4):
            for z in range(4):
                zz = turn(zh, rel[z])
                want = zz * 16 + (turn(y, rel[r]) * 4 + x if q == 0 else y * 4 + turn(x, rel[r]))
                rows = jnp.sum(jnp.where(lane64 == want, zr, 0.0), axis=1, keepdims=True)
                t = rows * kx * (1.0 / 1024.0)
                even, odd = cas_dcas(t)
                tab[q, r, z, 0] = even
                tab[q, r, z, 1] = odd * fx

    for q in range(2):
        gat[q, 0].wait_recv()
        gat[q, 4] = start(ag.at[q, 0, 1], ag.at[q, 0, 3], AG + 6 * q + 4, first[q](1))
    for q in range(2):
        gat[q, 3].wait_recv()
        gat[q, 5] = start(ag.at[q, 1, 2], ag.at[q, 1, 3], AG + 6 * q + 5, first[q](-1))

    def fill_e(i, _):
        row = pl.multiple_of(i * 32, 32)
        a = (row + iota((32, 1), 0)).astype(F32)
        c = iota((1, 512), 1).astype(F32)
        co, si = cos_sin(a * c * (1.0 / 128.0))
        for k, value in enumerate((co, si)):
            hi, lo = split(value)
            e_hi[pl.ds(row, 32), k * 512 : (k + 1) * 512] = hi
            e_lo[pl.ds(row, 32), k * 512 : (k + 1) * 512] = lo
        return 0

    lax.fori_loop(0, 16, fill_e, 0)

    def fill_p(i, _):
        row = pl.multiple_of(i * 32, 32)
        a = row + iota((32, 1024), 0)
        b = iota((32, 1024), 1)
        perm[pl.ds(row, 32), :] = jnp.where(a == 8 * (b % 128) + b // 128, 1.0, 0.0).astype(BF16)
        return 0

    lax.fori_loop(0, 32, fill_p, 0)

    near, mid = {}, {}
    for q in range(2):
        for k in (1, 2, 4, 5):
            gat[q, k].wait_recv()
        table = tab[q]
        both = split(table.reshape(256, 256))
        even = split(table[:, :, 0].reshape(128, 256))
        acc = dot3(both, split(ag[q, 0].reshape(256, 512)))
        ps[q, :, :, 0:2] = acc.reshape(4, 4, 2, 8, 512)
        acc = dot3(even, split(ag[q, 1].reshape(256, 512)))
        ps[q, :, :, 2] = acc.reshape(4, 4, 8, 512)
        b = RS + 6 * q
        right, left = second[q](1), second[q](-1)
        near[q, 0] = start(ps.at[q, 3, pl.ds(0, 2)], ob.at[q, 0], b, right)
        near[q, 1] = start(ps.at[q, 3, pl.ds(2, 2)], ob.at[q, 1], b + 1, left)
        near[q, 2] = start(ps.at[q, 1, pl.ds(2, 2)], nb.at[q, 0, pl.ds(2, 2)], b + 2, right)
        near[q, 3] = start(ps.at[q, 2, pl.ds(0, 2)], nb.at[q, 1, pl.ds(0, 2)], b + 3, left)
    for q in range(2):
        b = RS + 6 * q
        right, left = second[q](1), second[q](-1)
        near[q, 0].wait_recv()
        ps[q, 1, 0:2] = ps[q, 1, 0:2] + ob[q, 0]
        near[q, 4] = start(ps.at[q, 1, pl.ds(0, 2)], nb.at[q, 0, pl.ds(0, 2)], b + 4, right)
        near[q, 1].wait_recv()
        ps[q, 2, 2:4] = ps[q, 2, 2:4] + ob[q, 1]
        near[q, 5] = start(ps.at[q, 2, pl.ds(2, 2)], nb.at[q, 1, pl.ds(2, 2)], b + 5, left)

    to_next, to_prev = (s_next, g), (s_prev, g)
    raw.append(start(vol.at[7], planes.at[0], RAW + 4, to_next))
    raw.append(start(spd.at[7], planes.at[1], RAW + 5, to_next))
    raw.append(start(lft.at[7], planes.at[2], RAW + 6, to_next))
    raw.append(start(lft.at[0], planes.at[3], RAW + 7, to_prev))

    right, left = on_z(1), on_z(-1)
    for q in range(2):
        for k in (2, 3, 4, 5):
            near[q, k].wait_recv()
        zs[q] = ps[q, 0] + nb[q, 0] + nb[q, 1]
        b = RZ + 3 * q
        ahead, back = (right, left) if q == 0 else (left, right)
        fore, aft = (1, 2) if q == 0 else (2, 1)
        mid[q, 0] = start(zs.at[q, 3], zo.at[q], b, ahead)
        mid[q, 1] = start(zs.at[q, aft], zn.at[q, 1], b + 1, back)
    for q in range(2):
        b = RZ + 3 * q
        ahead = right if q == 0 else left
        fore = 1 if q == 0 else 2
        mid[q, 0].wait_recv()
        zs[q, fore] = zs[q, fore] + zo[q]
        mid[q, 2] = start(zs.at[q, fore], zn.at[q, 0], b + 2, ahead)
    for q in range(2):
        mid[q, 1].wait_recv()
        mid[q, 2].wait_recv()
        xp[:, :, q * 512 : (q + 1) * 512] = zs[q, 0] + zn[q, 0] + zn[q, 1]

    hi, lo = split(xp[...].reshape(24, 1024))
    moved = dot(hi, perm[...]) + dot(lo, perm[...])
    moved = moved.reshape(3, 8, 1024)
    xg[g] = moved
    sub = iota((8, 1024), 0)
    count = jnp.full((8, 1024), zc_ref[0].astype(F32))
    head = jnp.where(sub == 6, count, 0.0)
    tail = jnp.where(sub == 7, count, 0.0)
    for k in range(3):
        head = jnp.where(sub == k, moved[k, 7:8], head)
        tail = jnp.where(sub == 3 + k, moved[k, 0:1], tail)
    hmsg[0] = head
    hmsg[1] = tail
    last = []
    for j in (1, 2, 3):
        last.append(start(xg.at[g], xg.at[g], GA + j - 1, (s, girth(j))))
    for j in range(4):
        last.append(start(hmsg.at[0], hp.at[g], HP + j, (s_next, girth(j))))
        last.append(start(hmsg.at[1], hn.at[g], HN + j, (s_prev, girth(j))))
    for c in last:
        c.wait_recv()

    for gg in range(4):
        halo = hp[gg] + hn[gg]
        for b in range(8):
            ks = slice(128 * b, 128 * (b + 1))
            os = slice(128 * gg, 128 * (gg + 1))
            ky = (1024 * gg + b + 8 * iota((1, 128), 1)).astype(F32)
            fy = ky * (1.0 / 2048.0) - (2.0 if gg >= 2 else 0.0)
            top = xg[gg, 0, :, ks]
            edge = halo[:, ks]
            lhs[b, 0:8, os] = top
            lhs[b, 8:16, os] = xg[gg, 1, :, ks]
            lhs[b, 16:24, os] = xg[gg, 2, :, ks]
            lhs[b, 24:32, os] = edge
            lhs[b, 32:40, os] = top * fy
            lhs[b, 40:48, os] = edge * fy
    uu[...] = dot3(split(lhs[...].reshape(384, 512)), (e_hi[...], e_lo[...])).reshape(8, 48, 1024)

    q8 = iota((16, 128), 0).astype(F32)
    places = [(2 * g - 1, 384)] + [(2 * g + i // 4, 128 * (i % 4)) for i in range(8)] + [(2 * g + 2, 0)]
    b8 = iota((8, 128), 0)
    for i, (block, c0) in enumerate(places):
        c = c0 + iota((8, 128), 1)
        t = (b8 * c).astype(F32) * (1.0 / 1024.0) + (b8 * block).astype(F32) * 0.5
        even, odd = cas_dcas(t)
        out = [jnp.zeros((8, 128), F32) for _ in range(6)]
        for b in range(8):
            ev, od = even[b : b + 1], odd[b : b + 1]
            for k in range(6):
                re = uu[b, 8 * k : 8 * k + 8, c0 : c0 + 128]
                im = uu[b, 8 * k : 8 * k + 8, 512 + c0 : 512 + c0 + 128]
                out[k] = out[k] + (re * ev + im * od if k < 4 else re * od - im * ev)
        cs = slice(128 * i, 128 * (i + 1))
        for k in range(6):
            hh[k, :, cs] = out[k]

    def weights(plane, count):
        q_ = jnp.minimum((plane + 0.5) / count, 1.0)
        w_ = 1.0 - (jnp.exp(q_ * q_ * q_ * jnp.sqrt(q_)) - 1.0) / (math.e - 1.0)
        return jnp.where(plane < count, w_, 0.0)

    def put(planes_, cs, height, tilt_x, lift, tilt_y, w):
        rise = (1.0 + tilt_x * tilt_x + tilt_y * tilt_y) * lift
        parts = (0.5 + 8.0 * height, jnp.exp(-0.5 * height), w * rise, w)
        for i, plane in enumerate(planes_):
            for k in range(4):
                hr[plane, k : k + 1, cs] = parts[k][i : i + 1]

    own_w = weights(iota((8, 128), 0).astype(F32), jnp.full((8, 128), zc_ref[0].astype(F32)))
    prev_w = weights(jnp.full((1, 128), 7.0, F32), hp[0, 6:7, 0:128])
    next_w = weights(jnp.full((1, 128), 0.0, F32), hn[0, 7:8, 0:128])
    for i in range(10):
        cs = slice(128 * i, 128 * (i + 1))
        put(range(8), cs, hh[0, :, cs], hh[1, :, cs], hh[2, :, cs], hh[4, :, cs], own_w)
        put((8,), cs, hh[3, 0:1, cs], hh[3, 1:2, cs], hh[3, 2:3, cs], hh[5, 0:1, cs], prev_w)
        put((9,), cs, hh[3, 3:4, cs], hh[3, 4:5, cs], hh[3, 5:6, cs], hh[5, 3:4, cs], next_w)

    for c in raw:
        c.wait_recv()
    for c in sent:
        c.wait_send()


def wave_part(zr, zone_count, eta, phi, vol, lft, spd):
    vmem = pl.BlockSpec(memory_space=pltpu.VMEM)
    anyw = pl.BlockSpec(memory_space=pl.ANY)
    return pl.pallas_call(
        wave_kernel,
        out_shape=(
            jax.ShapeDtypeStruct((10, 4, EXT), F32),
            jax.ShapeDtypeStruct((4, 48, 1024), F32),
            jax.ShapeDtypeStruct((4, 8, 48, 128), F32),
        ),
        in_specs=[vmem, pl.BlockSpec(memory_space=pltpu.SMEM), vmem, vmem, anyw, anyw, anyw],
        out_specs=(vmem, anyw, anyw),
        scratch_shapes=[
            pltpu.VMEM((2, 2, 4, 64, 512), F32),
            pltpu.VMEM((2, 4, 4, 2, 8, 256), F32),
            pltpu.VMEM((2, 4, 4, 3, 8, 512), F32),
            pltpu.VMEM((2, 2, 2, 3, 8, 512), F32),
            pltpu.VMEM((2, 2, 4, 3, 8, 512), F32),
            pltpu.VMEM((2, 4, 3, 8, 512), F32),
            pltpu.VMEM((2, 3, 8, 512), F32),
            pltpu.VMEM((2, 2, 3, 8, 512), F32),
            pltpu.VMEM((4, 3, 8, 1024), F32),
            pltpu.VMEM((3, 8, 1024), F32),
            pltpu.VMEM((2, 8, 1024), F32),
            pltpu.VMEM((4, 8, 1024), F32),
            pltpu.VMEM((4, 8, 1024), F32),
            pltpu.VMEM((512, 1024), BF16),
            pltpu.VMEM((512, 1024), BF16),
            pltpu.VMEM((1024, 1024), BF16),
            pltpu.VMEM((8, 48, 512), F32),
            pltpu.VMEM((8, 48, 1024), F32),
            pltpu.VMEM((6, 8, EXT), F32),
            pltpu.SemaphoreType.DMA((N_SEM,)),
            pltpu.SemaphoreType.DMA((N_SEM,)),
        ],
        compiler_params=pltpu.CompilerParams(
            collective_id=0, has_side_effects=True, vmem_limit_bytes=40 * 1024 * 1024
        ),
        name="wave_part",
    )(zr, zone_count, eta, phi, vol, lft, spd)


def field_kernel(marks, hr, planes, cols, vol, lft, spd, vol_out, lft_out, rv, rl, fx):
    t = pl.program_id(0)
    s = lax.axis_index("stream")
    g = lax.axis_index("girth")
    level8 = iota((48, 128), 0).astype(F32) - 23.5
    rise_z = jnp.exp(level8 * 0.0625)
    lane = iota((48, 128), 1)
    row = iota((48, 128), 0)

    def surface(plane, i):
        cs = slice(128 * i, 128 * (i + 1))
        return [hr[plane, k : k + 1, cs] for k in range(4)]

    def relax_v(v, here):
        goal = jnp.clip(here[0] - level8, 0.0, 1.0)
        return here[3] * goal + (1.0 - here[3]) * v

    def relax_l(l, here):
        return here[2] * jnp.minimum(rise_z * here[1], 1.0) + (1.0 - here[3]) * l

    def group(i):
        return slice(128 * i, 128 * (i + 1))

    now = lax.rem(t, 3)
    one = lax.rem(t + 2, 3)
    two = lax.rem(t + 1, 3)

    @pl.when(t < 8)
    def _():
        for i in range(8):
            here = surface(t, i + 1)
            v = relax_v(vol[0, :, group(i)], here)
            rv[now, :, group(i)] = v
            fx[now, :, group(i)] = spd[0, :, group(i)] * v
            rl[now, :, group(i)] = relax_l(lft[0, :, group(i)], here)

    @pl.when(t == 0)
    def _():
        for i in range(8):
            here = surface(8, i + 1)
            v = relax_v(planes[0, :, group(i)], here)
            l = relax_l(planes[2, :, group(i)], here)
            fx[2, :, group(i)] = jnp.where(s > 0, planes[1, :, group(i)] * v, 0.0)
            rl[2, :, group(i)] = jnp.where(s > 0, l, 0.0)

    @pl.when(t == 8)
    def _():
        for i in range(8):
            l = relax_l(planes[3, :, group(i)], surface(9, i + 1))
            rl[2, :, group(i)] = jnp.where(s < 63, l, 0.0)

    @pl.when(t >= 1)
    def _():
        u = t - 1
        mark2 = jnp.concatenate(
            [jnp.full((8, 128), 2.0 * marks[u, k].astype(F32), F32) for k in range(6)], axis=0
        )
        here = surface(u, 0)
        v_left = jnp.where(g > 0, relax_v(cols[0, u], here), 0.0)
        l_left = jnp.where(g > 0, relax_l(cols[1, u], here), 0.0)
        here = surface(u, 9)
        v_right = jnp.where(g < 3, relax_v(cols[2, u], here), 0.0)
        l_right = jnp.where(g < 3, relax_l(cols[3, u], here), 0.0)
        v = rv[one, :, group(0)]
        l = rl[one, :, group(0)]
        v_fore, l_fore = pltpu.roll(v_left, 1, 1), pltpu.roll(l_left, 1, 1)
        v_back, l_back = pltpu.roll(v, 127, 1), pltpu.roll(l, 127, 1)
        for i in range(8):
            if i < 7:
                v_then, l_then = rv[one, :, group(i + 1)], rl[one, :, group(i + 1)]
            else:
                v_then, l_then = v_right, l_right
            v_fore_own, l_fore_own = pltpu.roll(v, 1, 1), pltpu.roll(l, 1, 1)
            v_back_then, l_back_then = pltpu.roll(v_then, 127, 1), pltpu.roll(l_then, 127, 1)
            v_y = jnp.where(lane == 0, v_fore, v_fore_own) + jnp.where(lane == 127, v_back_then, v_back)
            l_y = jnp.where(lane == 0, l_fore, l_fore_own) + jnp.where(lane == 127, l_back_then, l_back)
            face = jnp.maximum(l, 0.0) * v + jnp.minimum(l, 0.0) * pltpu.roll(v, 47, 0)
            face = jnp.where(row == 47, 0.0, face)
            div = face - pltpu.roll(face, 1, 0)
            upwind = fx[one, :, group(i)] - fx[two, :, group(i)]
            sharpen = mark2 * (v * (1.0 - v) * (2.0 * v - 1.0))
            vol_out[0, :, group(i)] = v - 0.3 * (upwind + div) + 0.1 * (v_y - 2.0 * v) + sharpen
            l_z = jnp.where(row == 47, 0.0, pltpu.roll(l, 47, 0)) + jnp.where(row == 0, 0.0, pltpu.roll(l, 1, 0))
            l_x = rl[now, :, group(i)] + rl[two, :, group(i)]
            lft_out[0, :, group(i)] = l + 0.15 * (l_x + l_y + l_z - 6.0 * l)
            v, l = v_then, l_then
            v_fore, l_fore, v_back, l_back = v_fore_own, l_fore_own, v_back_then, l_back_then


def field_part(marks, hr, planes, cols, vol, lft, spd):
    vmem = pl.BlockSpec(memory_space=pltpu.VMEM)
    plane = pl.BlockSpec((1, 48, 1024), lambda t: (jnp.minimum(t, 7), 0, 0))
    out = pl.BlockSpec((1, 48, 1024), lambda t: (jnp.maximum(t - 1, 0), 0, 0))
    return pl.pallas_call(
        field_kernel,
        grid=(9,),
        out_shape=(jax.ShapeDtypeStruct((8, 48, 1024), F32),) * 2,
        in_specs=[pl.BlockSpec(memory_space=pltpu.SMEM), vmem, vmem, vmem, plane, plane, plane],
        out_specs=(out, out),
        scratch_shapes=[pltpu.VMEM((3, 48, 1024), F32)] * 3,
        compiler_params=pltpu.CompilerParams(vmem_limit_bytes=32 * 1024 * 1024),
        name="field_part",
    )(marks, hr, planes, cols, vol, lft, spd)


def on_device(eta_hat, phi_hat, zone_rows, zone_count, volume, lift, stream_speed, surface_blocks):
    hr, planes, cols = wave_part(zone_rows.T, zone_count, eta_hat, phi_hat, volume, lift, stream_speed)
    return field_part(surface_blocks, hr, planes, cols, volume, lift, stream_speed)


def solution(mesh):
    return jax.shard_map(
        on_device,
        mesh=mesh,
        in_specs=(
            P("stream", "girth"),
            P("stream", "girth"),
            P(),
            P("stream"),
            P("stream", None, "girth"),
            P("stream", None, "girth"),
            P("stream", None, "girth"),
            P("stream", None),
        ),
        out_specs=(P("stream", None, "girth"), P("stream", None, "girth")),
        check_vma=False,
    )
```

time: 590 us -> 89.7 us (0.15)
  the two profiles are of different devices: /device:TPU:31 before, /device:TPU:33 now
where the time goes in v1:
time: 89.7 us; the launch traced here: 88.5 us
  Pallas kernels  80.4 us (90%)
  local copies, waits for them, and re-layouts  6.8 us (8%)
  between operations  1.31 us (1%)
    pallas_call x1, Pallas kernels, wave_part(): pl.pallas_call(wave_kernel, out_shape=(jax.ShapeDtypeStruct((10, 4, EXT),...  74.2 us
    unnamed x14, local copies, waits for them, and re-layouts  6.8 us
    pallas_call x1, Pallas kernels, field_part(): pl.pallas_call(field_kernel, grid=(9,), out_shape=(jax.ShapeDtypeStruct((...  6.21 us

profile of v1, /device:TPU:33, one launch (start us, length us, event | category | flops | bytes accessed | tf_op | source)
XLA Modules:
  0.0 88.5 jit_solution(2928551633121472186)
XLA Ops:
  1.3 0.0 copy-start
  1.3 1.4 %copy-done = f32[8,48,1024]{2,1,0:T(8,128)S(1)} copy-done((f32[8,48,1024]{2,1,0:T(8,128)S(1)}, f32[8,48,1024]{2,1,0:T(8,128)}, u32[]{:S(2)}) %copy-start) | copy-done | bytes 1572888
  2.7 0.0 copy-start.1
  2.7 1.4 %copy-done.1 = f32[8,48,1024]{2,1,0:T(8,128)S(1)} copy-done((f32[8,48,1024]{2,1,0:T(8,128)S(1)}, f32[8,48,1024]{2,1,0:T(8,128)}, u32[]{:S(2)}) %copy-start.1) | copy-done | bytes 1572888
  4.1 0.0 copy-start.2
  4.1 1.4 %copy-done.2 = f32[8,48,1024]{2,1,0:T(8,128)S(1)} copy-done((f32[8,48,1024]{2,1,0:T(8,128)S(1)}, f32[8,48,1024]{2,1,0:T(8,128)}, u32[]{:S(2)}) %copy-start.2) | copy-done | bytes 1572888
  5.5 0.0 copy-start.3
  5.5 0.9 %copy-done.3 = f32[64,1024]{1,0:T(8,128)S(1)} copy-done((f32[64,1024]{1,0:T(8,128)S(1)}, f32[64,1024]{1,0:T(8,128)}, u32[]{:S(2)}) %copy-start.3) | copy-done | bytes 262168
  6.5 0.0 copy-start.4
  6.5 0.9 %copy-done.4 = f32[64,1024]{1,0:T(8,128)S(1)} copy-done((f32[64,1024]{1,0:T(8,128)S(1)}, f32[64,1024]{1,0:T(8,128)}, u32[]{:S(2)}) %copy-start.4) | copy-done | bytes 262168
  7.4 0.0 copy-start.5
  7.4 0.7 copy-done.5
  8.1 0.0 copy-start.6
  8.1 74.2 %wave_part.1 = (f32[10,4,1280]{2,1,0:T(4,128)S(1)}, f32[4,48,1024]{2,1,0:T(8,128)S(1)}, f32[4,8,48,128]{3,2,1,0:T(8,128)S(1)}) custom-call(s32[8,64]{1,0:T(8,128)S(1)} %bitcast.1, s32[1]{0:T(128)S(6)} %copy.10.zc_ref, f32[64,1024]{1,0:T(8,128)S(1)} %copy-done.3, f32[64,1024]{1,0:T(8,128)S(1)} %copy-done.4, f32[8,48,1024]{2,1,0:T(8,128)S(1)} %copy-done, ...), custom_call_target="tpu_custom_call" | custom-call | tf_op jit(solution)/shard_map/wave_part/pallas_call | solution.py:350
  82.3 0.0 copy-done.6
  82.3 6.2 %field_part.1 = (f32[8,48,1024]{2,1,0:T(8,128)}, f32[8,48,1024]{2,1,0:T(8,128)}) custom-call(s32[8,6]{1,0:T(8,128)S(1)} %copy-done.6, f32[10,4,1280]{2,1,0:T(4,128)S(1)} %get-tuple-element.5.hr, f32[4,48,1024]{2,1,0:T(8,128)S(1)} %get-tuple-element.6.planes, f32[4,8,48,128]{3,2,1,0:T(8,128)S(1)} %get-tuple-element.7.cols, f32[8,48,1024]{2,1,0:T(8,128)S(1)} %copy-done, ...), custom_call_target="tpu_custom_call" | custom-call | tf_op jit(solution)/shard_map/field_part/pallas_call | solution.py:482
Async XLA Ops:
  1.3 1.4 %copy-start = (f32[8,48,1024]{2,1,0:T(8,128)S(1)}, f32[8,48,1024]{2,1,0:T(8,128)}, u32[]{:S(2)}) copy-start(f32[8,48,1024]{2,1,0:T(8,128)} %vol.3) | copy-start | bytes 4718596
  2.7 1.4 %copy-start.1 = (f32[8,48,1024]{2,1,0:T(8,128)S(1)}, f32[8,48,1024]{2,1,0:T(8,128)}, u32[]{:S(2)}) copy-start(f32[8,48,1024]{2,1,0:T(8,128)} %lft.3) | copy-start | bytes 4718596
  4.1 1.4 %copy-start.2 = (f32[8,48,1024]{2,1,0:T(8,128)S(1)}, f32[8,48,1024]{2,1,0:T(8,128)}, u32[]{:S(2)}) copy-start(f32[8,48,1024]{2,1,0:T(8,128)} %spd.3) | copy-start | bytes 4718596
  5.5 0.9 %copy-start.3 = (f32[64,1024]{1,0:T(8,128)S(1)}, f32[64,1024]{1,0:T(8,128)}, u32[]{:S(2)}) copy-start(f32[64,1024]{1,0:T(8,128)} %eta.1) | copy-start | bytes 786436
  6.5 0.9 %copy-start.4 = (f32[64,1024]{1,0:T(8,128)S(1)}, f32[64,1024]{1,0:T(8,128)}, u32[]{:S(2)}) copy-start(f32[64,1024]{1,0:T(8,128)} %phi.1) | copy-start | bytes 786436
  7.4 0.7 copy-start.5
  8.1 74.2 %copy-start.6 = (s32[8,6]{1,0:T(8,128)S(1)}, s32[8,6]{1,0:T(8,128)}, u32[]{:S(2)}) copy-start(s32[8,6]{1,0:T(8,128)} %marks.1) | copy-start | bytes 580

commit v2 on v1

--- a/solution.py
+++ b/solution.py
@@ -12,8 +12,8 @@
 MESH = pl.DeviceIdType.MESH
 EXT = 1280
 
-AG, RS, RZ, GA, HP, HN, RAW = 0, 12, 24, 30, 33, 37, 41
-N_SEM = 49
+AG, RS, RZ, GA, ROWS, COLS, PLANES, RELAY = 0, 12, 24, 30, 33, 35, 39, 43
+N_SEM = 47
 
 
 def iota(shape, dim):
@@ -71,10 +71,10 @@
 
 
 def wave_kernel(
-    zr_ref, zc_ref, eta, phi, vol, lft, spd,
+    zr_hbm, zc_ref, eta, phi_hbm, vol, lft, spd,
     hr, planes, cols,
-    ag, tab, ps, ob, nb, zs, zo, zn, xg, xp, hmsg, hp, hn, e_hi, e_lo, perm, lhs, uu, hh,
-    ssem, rsem,
+    ag, tab, ps, ob, nb, zs, zo, zn, xg, xp, e_hi, e_lo, perm, lhs, uu, hh, relay, zr_ref, phi,
+    ssem, rsem, lsem,
 ):
     s = lax.axis_index("stream")
     g = lax.axis_index("girth")
@@ -95,6 +95,15 @@
     def on_z(d):
         return at(turn(zh, d), y, x)
 
+    fetched = [
+        pltpu.make_async_copy(eta.at[:, pl.ds(0, 512)], ag.at[0, 0, 0], lsem.at[0]),
+        pltpu.make_async_copy(eta.at[:, pl.ds(512, 512)], ag.at[1, 0, 0], lsem.at[1]),
+        pltpu.make_async_copy(phi_hbm, phi, lsem.at[2]),
+        pltpu.make_async_copy(zr_hbm, zr_ref, lsem.at[3]),
+    ]
+    for c in fetched:
+        c.start()
+
     s_next = lax.rem(s + 1, 64)
     s_prev = lax.rem(s + 63, 64)
 
@@ -103,8 +112,7 @@
 
     targets = [on_x(1), on_x(-1), on_y(1), on_y(-1), on_z(1), on_z(-1)]
     targets += [(s, girth(j)) for j in (1, 2, 3)]
-    targets += [(s_next, girth(j)) for j in range(4)]
-    targets += [(s_prev, girth(j)) for j in range(4)]
+    targets += [(s_next, g), (s_prev, g), at(zh, 3 - y, 3 - x)]
     barrier = pltpu.get_barrier_semaphore()
     for device in targets:
         pl.semaphore_signal(barrier, inc=1, device_id=device, device_id_type=MESH)
@@ -129,10 +137,27 @@
 
     gat = {}
     for q in range(2):
-        cs = pl.ds(q * 512, 512)
-        ag[q, 0, 0] = eta[:, cs]
+        fetched[q].wait()
         gat[q, 0] = start(ag.at[q, 0, 0], ag.at[q, 0, 1], AG + 6 * q, first[q](1))
         gat[q, 1] = start(ag.at[q, 0, 0], ag.at[q, 0, 2], AG + 6 * q + 1, first[q](-1))
+    high_edge = jnp.logical_and(x == 3, y == 3)
+    low_edge = jnp.logical_and(x == 0, y == 0)
+
+    up = [
+        copy(f.at[7], relay.at[k], RELAY + k, on_z(1)) for k, f in enumerate((vol, spd, lft))
+    ]
+    down = copy(lft.at[0], relay.at[0], RELAY + 3, on_z(-1))
+
+    @pl.when(high_edge)
+    def _():
+        for c in up:
+            c.start()
+
+    @pl.when(low_edge)
+    def _():
+        down.start()
+
+    fetched[2].wait()
     kx_own = (s * 64 + iota((64, 1), 0)).astype(F32)
     fx_own = kx_own / 2048.0 - jnp.where(kx_own >= 2048.0, 2.0, 0.0)
     for q in range(2):
@@ -147,11 +172,12 @@
     raw = []
     edge_left, edge_right = pl.ds(0, 128), pl.ds(896, 128)
     to_right, to_left = (s, girth(1)), (s, girth(3))
-    raw.append(start(vol.at[:, :, edge_right], cols.at[0], RAW, to_right))
-    raw.append(start(lft.at[:, :, edge_right], cols.at[1], RAW + 1, to_right))
-    raw.append(start(vol.at[:, :, edge_left], cols.at[2], RAW + 2, to_left))
-    raw.append(start(lft.at[:, :, edge_left], cols.at[3], RAW + 3, to_left))
-
+    raw.append(start(vol.at[:, :, edge_right], cols.at[0], COLS, to_right))
+    raw.append(start(lft.at[:, :, edge_right], cols.at[1], COLS + 1, to_right))
+    raw.append(start(vol.at[:, :, edge_left], cols.at[2], COLS + 2, to_left))
+    raw.append(start(lft.at[:, :, edge_left], cols.at[3], COLS + 3, to_left))
+
+    fetched[3].wait()
     zr = zr_ref[...].astype(F32)
     lane64 = iota((8, 64), 1)
     lane256 = iota((1, 256), 1)
@@ -232,11 +258,30 @@
         ps[q, 2, 2:4] = ps[q, 2, 2:4] + ob[q, 1]
         near[q, 5] = start(ps.at[q, 2, pl.ds(2, 2)], nb.at[q, 1, pl.ds(2, 2)], b + 5, left)
 
-    to_next, to_prev = (s_next, g), (s_prev, g)
-    raw.append(start(vol.at[7], planes.at[0], RAW + 4, to_next))
-    raw.append(start(spd.at[7], planes.at[1], RAW + 5, to_next))
-    raw.append(start(lft.at[7], planes.at[2], RAW + 6, to_next))
-    raw.append(start(lft.at[0], planes.at[3], RAW + 7, to_prev))
+    onward = [copy(f.at[7], planes.at[k], PLANES + k, (s_next, g)) for k, f in enumerate((vol, spd, lft))]
+    onward_far = [copy(relay.at[k], planes.at[k], PLANES + k, at(zh, 0, 0)) for k in range(3)]
+    backward = copy(lft.at[0], planes.at[3], PLANES + 3, (s_prev, g))
+    backward_far = copy(relay.at[0], planes.at[3], PLANES + 3, at(zh, 3, 3))
+
+    @pl.when(high_edge)
+    def _():
+        for k in range(3):
+            up[k].wait_recv()
+            onward_far[k].start()
+
+    @pl.when(jnp.logical_not(high_edge))
+    def _():
+        for c in onward:
+            c.start()
+
+    @pl.when(low_edge)
+    def _():
+        down.wait_recv()
+        backward_far.start()
+
+    @pl.when(jnp.logical_not(low_edge))
+    def _():
+        backward.start()
 
     right, left = on_z(1), on_z(-1)
     for q in range(2):
@@ -264,84 +309,84 @@
     moved = dot(hi, perm[...]) + dot(lo, perm[...])
     moved = moved.reshape(3, 8, 1024)
     xg[g] = moved
-    sub = iota((8, 1024), 0)
-    count = jnp.full((8, 1024), zc_ref[0].astype(F32))
-    head = jnp.where(sub == 6, count, 0.0)
-    tail = jnp.where(sub == 7, count, 0.0)
-    for k in range(3):
-        head = jnp.where(sub == k, moved[k, 7:8], head)
-        tail = jnp.where(sub == 3 + k, moved[k, 0:1], tail)
-    hmsg[0] = head
-    hmsg[1] = tail
     last = []
     for j in (1, 2, 3):
         last.append(start(xg.at[g], xg.at[g], GA + j - 1, (s, girth(j))))
-    for j in range(4):
-        last.append(start(hmsg.at[0], hp.at[g], HP + j, (s_next, girth(j))))
-        last.append(start(hmsg.at[1], hn.at[g], HN + j, (s_prev, girth(j))))
     for c in last:
         c.wait_recv()
 
     for gg in range(4):
-        halo = hp[gg] + hn[gg]
+        os = slice(128 * gg, 128 * (gg + 1))
         for b in range(8):
             ks = slice(128 * b, 128 * (b + 1))
-            os = slice(128 * gg, 128 * (gg + 1))
             ky = (1024 * gg + b + 8 * iota((1, 128), 1)).astype(F32)
             fy = ky * (1.0 / 2048.0) - (2.0 if gg >= 2 else 0.0)
             top = xg[gg, 0, :, ks]
-            edge = halo[:, ks]
             lhs[b, 0:8, os] = top
             lhs[b, 8:16, os] = xg[gg, 1, :, ks]
             lhs[b, 16:24, os] = xg[gg, 2, :, ks]
-            lhs[b, 24:32, os] = edge
-            lhs[b, 32:40, os] = top * fy
-            lhs[b, 40:48, os] = edge * fy
-    uu[...] = dot3(split(lhs[...].reshape(384, 512)), (e_hi[...], e_lo[...])).reshape(8, 48, 1024)
-
-    q8 = iota((16, 128), 0).astype(F32)
+            lhs[b, 24:32, os] = top * fy
+    uu[...] = dot3(split(lhs[...].reshape(256, 512)), (e_hi[...], e_lo[...])).reshape(8, 32, 1024)
+
     places = [(2 * g - 1, 384)] + [(2 * g + i // 4, 128 * (i % 4)) for i in range(8)] + [(2 * g + 2, 0)]
     b8 = iota((8, 128), 0)
     for i, (block, c0) in enumerate(places):
         c = c0 + iota((8, 128), 1)
         t = (b8 * c).astype(F32) * (1.0 / 1024.0) + (b8 * block).astype(F32) * 0.5
         even, odd = cas_dcas(t)
-        out = [jnp.zeros((8, 128), F32) for _ in range(6)]
+        out = [jnp.zeros((8, 128), F32) for _ in range(4)]
         for b in range(8):
             ev, od = even[b : b + 1], odd[b : b + 1]
-            for k in range(6):
+            for k in range(4):
                 re = uu[b, 8 * k : 8 * k + 8, c0 : c0 + 128]
                 im = uu[b, 8 * k : 8 * k + 8, 512 + c0 : 512 + c0 + 128]
-                out[k] = out[k] + (re * ev + im * od if k < 4 else re * od - im * ev)
+                out[k] = out[k] + (re * ev + im * od if k < 3 else re * od - im * ev)
         cs = slice(128 * i, 128 * (i + 1))
-        for k in range(6):
+        for k in range(4):
             hh[k, :, cs] = out[k]
 
-    def weights(plane, count):
-        q_ = jnp.minimum((plane + 0.5) / count, 1.0)
-        w_ = 1.0 - (jnp.exp(q_ * q_ * q_ * jnp.sqrt(q_)) - 1.0) / (math.e - 1.0)
-        return jnp.where(plane < count, w_, 0.0)
-
-    def put(planes_, cs, height, tilt_x, lift, tilt_y, w):
+    plane = iota((8, 128), 0).astype(F32)
+    count = jnp.full((8, 128), zc_ref[0].astype(F32))
+    q_ = jnp.minimum((plane + 0.5) / count, 1.0)
+    w = 1.0 - (jnp.exp(q_ * q_ * q_ * jnp.sqrt(q_)) - 1.0) / (math.e - 1.0)
+    w = jnp.where(plane < count, w, 0.0)
+    for i in range(10):
+        cs = slice(128 * i, 128 * (i + 1))
+        height, tilt_x, lift, tilt_y = (hh[k, :, cs] for k in range(4))
         rise = (1.0 + tilt_x * tilt_x + tilt_y * tilt_y) * lift
         parts = (0.5 + 8.0 * height, jnp.exp(-0.5 * height), w * rise, w)
-        for i, plane in enumerate(planes_):
+        for p in range(8):
             for k in range(4):
-                hr[plane, k : k + 1, cs] = parts[k][i : i + 1]
-
-    own_w = weights(iota((8, 128), 0).astype(F32), jnp.full((8, 128), zc_ref[0].astype(F32)))
-    prev_w = weights(jnp.full((1, 128), 7.0, F32), hp[0, 6:7, 0:128])
-    next_w = weights(jnp.full((1, 128), 0.0, F32), hn[0, 7:8, 0:128])
-    for i in range(10):
-        cs = slice(128 * i, 128 * (i + 1))
-        put(range(8), cs, hh[0, :, cs], hh[1, :, cs], hh[2, :, cs], hh[4, :, cs], own_w)
-        put((8,), cs, hh[3, 0:1, cs], hh[3, 1:2, cs], hh[3, 2:3, cs], hh[5, 0:1, cs], prev_w)
-        put((9,), cs, hh[3, 3:4, cs], hh[3, 4:5, cs], hh[3, 5:6, cs], hh[5, 3:4, cs], next_w)
-
-    for c in raw:
+                hr[p, k : k + 1, cs] = parts[k][p : p + 1]
+
+    rows = [
+        start(hr.at[7], hr.at[8], ROWS, (s_next, g)),
+        start(hr.at[0], hr.at[9], ROWS + 1, (s_prev, g)),
+    ]
+
+    for c in raw + rows + onward + [backward]:
         c.wait_recv()
     for c in sent:
         c.wait_send()
+
+    @pl.when(high_edge)
+    def _():
+        for c in up + onward_far:
+            c.wait_send()
+
+    @pl.when(jnp.logical_not(high_edge))
+    def _():
+        for c in onward:
+            c.wait_send()
+
+    @pl.when(low_edge)
+    def _():
+        down.wait_send()
+        backward_far.wait_send()
+
+    @pl.when(jnp.logical_not(low_edge))
+    def _():
+        backward.wait_send()
 
 
 def wave_part(zr, zone_count, eta, phi, vol, lft, spd):
@@ -354,7 +399,7 @@
             jax.ShapeDtypeStruct((4, 48, 1024), F32),
             jax.ShapeDtypeStruct((4, 8, 48, 128), F32),
         ),
-        in_specs=[vmem, pl.BlockSpec(memory_space=pltpu.SMEM), vmem, vmem, anyw, anyw, anyw],
+        in_specs=[anyw, pl.BlockSpec(memory_space=pltpu.SMEM), anyw, anyw, anyw, anyw, anyw],
         out_specs=(vmem, anyw, anyw),
         scratch_shapes=[
             pltpu.VMEM((2, 2, 4, 64, 512), F32),
@@ -367,20 +412,21 @@
             pltpu.VMEM((2, 2, 3, 8, 512), F32),
             pltpu.VMEM((4, 3, 8, 1024), F32),
             pltpu.VMEM((3, 8, 1024), F32),
-            pltpu.VMEM((2, 8, 1024), F32),
-            pltpu.VMEM((4, 8, 1024), F32),
-            pltpu.VMEM((4, 8, 1024), F32),
             pltpu.VMEM((512, 1024), BF16),
             pltpu.VMEM((512, 1024), BF16),
             pltpu.VMEM((1024, 1024), BF16),
-            pltpu.VMEM((8, 48, 512), F32),
-            pltpu.VMEM((8, 48, 1024), F32),
-            pltpu.VMEM((6, 8, EXT), F32),
+            pltpu.VMEM((8, 32, 512), F32),
+            pltpu.VMEM((8, 32, 1024), F32),
+            pltpu.VMEM((4, 8, EXT), F32),
+            pltpu.VMEM((3, 48, 1024), F32),
+            pltpu.VMEM((8, 64), jnp.int32),
+            pltpu.VMEM((64, 1024), F32),
             pltpu.SemaphoreType.DMA((N_SEM,)),
             pltpu.SemaphoreType.DMA((N_SEM,)),
+            pltpu.SemaphoreType.DMA((4,)),
         ],
         compiler_params=pltpu.CompilerParams(
-            collective_id=0, has_side_effects=True, vmem_limit_bytes=40 * 1024 * 1024
+            collective_id=0, has_side_effects=True, vmem_limit_bytes=60 * 1024 * 1024
         ),
         name="wave_part",
     )(zr, zone_count, eta, phi, vol, lft, spd)
@@ -486,7 +532,7 @@
         in_specs=[pl.BlockSpec(memory_space=pltpu.SMEM), vmem, vmem, vmem, plane, plane, plane],
         out_specs=(out, out),
         scratch_shapes=[pltpu.VMEM((3, 48, 1024), F32)] * 3,
-        compiler_params=pltpu.CompilerParams(vmem_limit_bytes=32 * 1024 * 1024),
+        compiler_params=pltpu.CompilerParams(vmem_limit_bytes=60 * 1024 * 1024),
         name="field_part",
     )(marks, hr, planes, cols, vol, lft, spd)
 

time: 89.7 us -> 77.1 us (0.86); the launches traced: 88.5 us -> 76.9 us
  local copies, waits for them, and re-layouts: 6.8 us -> 0 us
  Pallas kernels: 80.4 us -> 75.6 us
    pallas_call x1, Pallas kernels: 74.2 us -> 66.6 us  [wave_part(): pl.pallas_call(wave_kernel, out_shape=(jax.ShapeDtypeStruct((10, 4, EXT),...]
    unnamed x14 -> x0, local copies, waits for them, and re-layouts: 6.8 us -> none
    pallas_call x1, Pallas kernels: 6.21 us -> 8.99 us  [field_part(): pl.pallas_call(field_kernel, grid=(9,), out_shape=(jax.ShapeDtypeStruct((...]
where the time goes in v2:
time: 77.1 us; the launch traced here: 76.9 us
  Pallas kernels  75.6 us (98%)
  between operations  1.28 us (2%)
    pallas_call x1, Pallas kernels, wave_part(): pl.pallas_call(wave_kernel, out_shape=(jax.ShapeDtypeStruct((10, 4, EXT),...  66.6 us
    pallas_call x1, Pallas kernels, field_part(): pl.pallas_call(field_kernel, grid=(9,), out_shape=(jax.ShapeDtypeStruct((...  8.99 us

profile of v2, /device:TPU:33, one launch (start us, length us, event | category | flops | bytes accessed | tf_op | source)
XLA Modules:
  0.0 76.9 jit_solution(6051696377082858893)
XLA Ops:
  1.3 66.6 %wave_part.1 = (f32[10,4,1280]{2,1,0:T(4,128)}, f32[4,48,1024]{2,1,0:T(8,128)}, f32[4,8,48,128]{3,2,1,0:T(8,128)}) custom-call(s32[8,64]{1,0:T(8,128)} %bitcast.1, s32[1]{0:T(128)S(6)} %copy.10.zc_ref, f32[64,1024]{1,0:T(8,128)} %eta.1, f32[64,1024]{1,0:T(8,128)} %phi_hbm.1, f32[8,48,1024]{2,1,0:T(8,128)} %vol.3, f32[8,48,1024]{2,1,0:T(8,128)} %lft.3, ...), custom_call_target="tpu_custom_call" | custom-call | tf_op jit(solution)/shard_map/wave_part/pallas_call | solution.py:395
  67.9 9.0 %field_part.1 = (f32[8,48,1024]{2,1,0:T(8,128)}, f32[8,48,1024]{2,1,0:T(8,128)}) custom-call(s32[8,6]{1,0:T(8,128)} %marks.1, f32[10,4,1280]{2,1,0:T(4,128)} %get-tuple-element.5.hr, f32[4,48,1024]{2,1,0:T(8,128)} %get-tuple-element.6.planes, f32[4,8,48,128]{3,2,1,0:T(8,128)} %get-tuple-element.7.cols, f32[8,48,1024]{2,1,0:T(8,128)} %vol.3, ...), custom_call_target="tpu_custom_call" | custom-call | tf_op jit(solution)/shard_map/field_part/pallas_call | solution.py:528

commit v3 on v2

--- a/solution.py
+++ b/solution.py
@@ -12,8 +12,8 @@
 MESH = pl.DeviceIdType.MESH
 EXT = 1280
 
-AG, RS, RZ, GA, ROWS, COLS, PLANES, RELAY = 0, 12, 24, 30, 33, 35, 39, 43
-N_SEM = 47
+AG, RS, RZ, GA, ROWS, COLS, PLANES, RELAY = 0, 12, 24, 30, 33, 35, 37, 41
+N_SEM = 46
 
 
 def iota(shape, dim):
@@ -71,10 +71,11 @@
 
 
 def wave_kernel(
-    zr_hbm, zc_ref, eta, phi_hbm, vol, lft, spd,
-    hr, planes, cols,
+    zr_hbm, zc_ref, marks, eta, phi_hbm, vol, lft, spd,
+    vol_out, lft_out,
+    hr, planes, cin, cmsg, ecol, vv, lv, sv, rv, rl, flux, ov, ol,
     ag, tab, ps, ob, nb, zs, zo, zn, xg, xp, e_hi, e_lo, perm, lhs, uu, hh, relay, zr_ref, phi,
-    ssem, rsem, lsem,
+    ssem, rsem, lsem, osem,
 ):
     s = lax.axis_index("stream")
     g = lax.axis_index("girth")
@@ -101,7 +102,17 @@
         pltpu.make_async_copy(phi_hbm, phi, lsem.at[2]),
         pltpu.make_async_copy(zr_hbm, zr_ref, lsem.at[3]),
     ]
-    for c in fetched:
+    edge_left, edge_right = pl.ds(0, 128), pl.ds(896, 128)
+    fields = [
+        pltpu.make_async_copy(vol.at[:, :, edge_right], ecol.at[0, 0], lsem.at[4]),
+        pltpu.make_async_copy(lft.at[:, :, edge_right], ecol.at[0, 1], lsem.at[5]),
+        pltpu.make_async_copy(vol.at[:, :, edge_left], ecol.at[1, 0], lsem.at[6]),
+        pltpu.make_async_copy(lft.at[:, :, edge_left], ecol.at[1, 1], lsem.at[7]),
+        pltpu.make_async_copy(vol, vv, lsem.at[8]),
+        pltpu.make_async_copy(lft, lv, lsem.at[9]),
+        pltpu.make_async_copy(spd, sv, lsem.at[10]),
+    ]
+    for c in fetched + fields:
         c.start()
 
     s_next = lax.rem(s + 1, 64)
@@ -143,9 +154,9 @@
     high_edge = jnp.logical_and(x == 3, y == 3)
     low_edge = jnp.logical_and(x == 0, y == 0)
 
-    up = [
-        copy(f.at[7], relay.at[k], RELAY + k, on_z(1)) for k, f in enumerate((vol, spd, lft))
-    ]
+    up = [copy(f.at[7], relay.at[k], RELAY + k, on_z(1)) for k, f in enumerate((vol, spd))]
+    across = copy(lft.at[7], relay.at[2], RELAY + 2, at(zh, 0, 0))
+    upward = copy(relay.at[2], planes.at[2], PLANES + 2, on_z(1))
     down = copy(lft.at[0], relay.at[0], RELAY + 3, on_z(-1))
 
     @pl.when(high_edge)
@@ -168,14 +179,6 @@
         ag[q, 1, 0] = rad * jnp.tanh(2.0 * rad) * phi[:, cs]
         gat[q, 2] = start(ag.at[q, 1, 0], ag.at[q, 1, 1], AG + 6 * q + 2, first[q](1))
         gat[q, 3] = start(ag.at[q, 1, 0], ag.at[q, 1, 2], AG + 6 * q + 3, first[q](-1))
-
-    raw = []
-    edge_left, edge_right = pl.ds(0, 128), pl.ds(896, 128)
-    to_right, to_left = (s, girth(1)), (s, girth(3))
-    raw.append(start(vol.at[:, :, edge_right], cols.at[0], COLS, to_right))
-    raw.append(start(lft.at[:, :, edge_right], cols.at[1], COLS + 1, to_right))
-    raw.append(start(vol.at[:, :, edge_left], cols.at[2], COLS + 2, to_left))
-    raw.append(start(lft.at[:, :, edge_left], cols.at[3], COLS + 3, to_left))
 
     fetched[3].wait()
     zr = zr_ref[...].astype(F32)
@@ -209,6 +212,20 @@
         gat[q, 3].wait_recv()
         gat[q, 5] = start(ag.at[q, 1, 2], ag.at[q, 1, 3], AG + 6 * q + 5, first[q](-1))
 
+    for c in fields[:4]:
+        c.wait()
+    lane = iota((48, 128), 1)
+    for side, at_lane in ((0, 127), (1, 0)):
+        packed = jnp.zeros((48, 128), F32)
+        for f in range(2):
+            for p in range(8):
+                packed = jnp.where(lane == 8 * f + p, ecol[side, f, p, :, at_lane : at_lane + 1], packed)
+        cmsg[side] = packed
+    raw = [
+        start(cmsg.at[0], cin.at[0], COLS, (s, girth(1))),
+        start(cmsg.at[1], cin.at[1], COLS + 1, (s, girth(3))),
+    ]
+
     def fill_e(i, _):
         row = pl.multiple_of(i * 32, 32)
         a = (row + iota((32, 1), 0)).astype(F32)
@@ -259,25 +276,18 @@
         near[q, 5] = start(ps.at[q, 2, pl.ds(2, 2)], nb.at[q, 1, pl.ds(2, 2)], b + 5, left)
 
     onward = [copy(f.at[7], planes.at[k], PLANES + k, (s_next, g)) for k, f in enumerate((vol, spd, lft))]
-    onward_far = [copy(relay.at[k], planes.at[k], PLANES + k, at(zh, 0, 0)) for k in range(3)]
+    onward_far = [copy(relay.at[k], planes.at[k], PLANES + k, at(zh, 0, 0)) for k in range(2)]
     backward = copy(lft.at[0], planes.at[3], PLANES + 3, (s_prev, g))
     backward_far = copy(relay.at[0], planes.at[3], PLANES + 3, at(zh, 3, 3))
 
     @pl.when(high_edge)
     def _():
-        for k in range(3):
-            up[k].wait_recv()
-            onward_far[k].start()
+        across.start()
 
     @pl.when(jnp.logical_not(high_edge))
     def _():
         for c in onward:
             c.start()
-
-    @pl.when(low_edge)
-    def _():
-        down.wait_recv()
-        backward_far.start()
 
     @pl.when(jnp.logical_not(low_edge))
     def _():
@@ -304,6 +314,19 @@
         mid[q, 1].wait_recv()
         mid[q, 2].wait_recv()
         xp[:, :, q * 512 : (q + 1) * 512] = zs[q, 0] + zn[q, 0] + zn[q, 1]
+
+    @pl.when(high_edge)
+    def _():
+        for k in range(2):
+            up[k].wait_recv()
+            onward_far[k].start()
+
+    @pl.when(low_edge)
+    def _():
+        down.wait_recv()
+        backward_far.start()
+        across.wait_recv()
+        upward.start()
 
     hi, lo = split(xp[...].reshape(24, 1024))
     moved = dot(hi, perm[...]) + dot(lo, perm[...])
@@ -364,14 +387,106 @@
         start(hr.at[0], hr.at[9], ROWS + 1, (s_prev, g)),
     ]
 
-    for c in raw + rows + onward + [backward]:
+    for c in fields[4:]:
+        c.wait()
+    level8 = iota((48, 128), 0).astype(F32) - 23.5
+    rise_z = jnp.exp(level8 * 0.0625)
+    row = iota((48, 128), 0)
+
+    def group(i):
+        return slice(128 * i, 128 * (i + 1))
+
+    def surface(plane, i):
+        return [hr[plane, k : k + 1, group(i)] for k in range(4)]
+
+    def relax_v(v, here):
+        goal = jnp.clip(here[0] - level8, 0.0, 1.0)
+        return here[3] * goal + (1.0 - here[3]) * v
+
+    def relax_l(l, here):
+        return here[2] * jnp.minimum(rise_z * here[1], 1.0) + (1.0 - here[3]) * l
+
+    def relax_plane(p, _):
+        for i in range(8):
+            here = surface(p, i + 1)
+            v = relax_v(vv[p, :, group(i)], here)
+            rv[p, :, group(i)] = v
+            flux[p + 1, :, group(i)] = sv[p, :, group(i)] * v
+            rl[p + 1, :, group(i)] = relax_l(lv[p, :, group(i)], here)
+        return 0
+
+    lax.fori_loop(0, 8, relax_plane, 0)
+    for c in raw:
         c.wait_recv()
+
+    def put_out(u):
+        return (
+            pltpu.make_async_copy(ov.at[u], vol_out.at[u], osem.at[0, u]),
+            pltpu.make_async_copy(ol.at[u], lft_out.at[u], osem.at[1, u]),
+        )
+
+    def step(n, _):
+        u = lax.rem(n + 1, 8)
+        mark2 = jnp.concatenate(
+            [jnp.full((8, 128), 2.0 * marks[u, k].astype(F32), F32) for k in range(6)], axis=0
+        )
+
+        def edge(side, f):
+            return jnp.sum(jnp.where(lane == u + 8 * f, cin[side], 0.0), axis=1, keepdims=True)
+
+        here = surface(u, 0)
+        v_left = jnp.where(g > 0, relax_v(edge(0, 0), here), 0.0)
+        l_left = jnp.where(g > 0, relax_l(edge(0, 1), here), 0.0)
+        here = surface(u, 9)
+        v_right = jnp.where(g < 3, relax_v(edge(1, 0), here), 0.0)
+        l_right = jnp.where(g < 3, relax_l(edge(1, 1), here), 0.0)
+        v = rv[u, :, group(0)]
+        l = rl[u + 1, :, group(0)]
+        v_fore, l_fore = pltpu.roll(v_left, 1, 1), pltpu.roll(l_left, 1, 1)
+        v_back, l_back = pltpu.roll(v, 127, 1), pltpu.roll(l, 127, 1)
+        for i in range(8):
+            if i < 7:
+                v_then, l_then = rv[u, :, group(i + 1)], rl[u + 1, :, group(i + 1)]
+            else:
+                v_then, l_then = v_right, l_right
+            v_fore_own, l_fore_own = pltpu.roll(v, 1, 1), pltpu.roll(l, 1, 1)
+            v_back_then, l_back_then = pltpu.roll(v_then, 127, 1), pltpu.roll(l_then, 127, 1)
+            v_y = jnp.where(lane == 0, v_fore, v_fore_own) + jnp.where(lane == 127, v_back_then, v_back)
+            l_y = jnp.where(lane == 0, l_fore, l_fore_own) + jnp.where(lane == 127, l_back_then, l_back)
+            face = jnp.maximum(l, 0.0) * v + jnp.minimum(l, 0.0) * pltpu.roll(v, 47, 0)
+            face = jnp.where(row == 47, 0.0, face)
+            div = face - pltpu.roll(face, 1, 0)
+            upwind = flux[u + 1, :, group(i)] - flux[u, :, group(i)]
+            sharpen = mark2 * (v * (1.0 - v) * (2.0 * v - 1.0))
+            ov[u, :, group(i)] = v - 0.3 * (upwind + div) + 0.1 * (v_y - 2.0 * v) + sharpen
+            l_z = jnp.where(row == 47, 0.0, pltpu.roll(l, 47, 0)) + jnp.where(row == 0, 0.0, pltpu.roll(l, 1, 0))
+            l_x = rl[u + 2, :, group(i)] + rl[u, :, group(i)]
+            ol[u, :, group(i)] = l + 0.15 * (l_x + l_y + l_z - 6.0 * l)
+            v, l = v_then, l_then
+            v_fore, l_fore, v_back, l_back = v_fore_own, l_fore_own, v_back_then, l_back_then
+        for c in put_out(u):
+            c.start()
+        return 0
+
+    lax.fori_loop(0, 6, step, 0)
+    for c in rows + onward + [backward]:
+        c.wait_recv()
+    for i in range(8):
+        here = surface(8, i + 1)
+        v = relax_v(planes[0, :, group(i)], here)
+        l = relax_l(planes[2, :, group(i)], here)
+        flux[0, :, group(i)] = jnp.where(s > 0, planes[1, :, group(i)] * v, 0.0)
+        rl[0, :, group(i)] = jnp.where(s > 0, l, 0.0)
+        l = relax_l(planes[3, :, group(i)], surface(9, i + 1))
+        rl[9, :, group(i)] = jnp.where(s < 63, l, 0.0)
+    lax.fori_loop(6, 8, step, 0)
+
     for c in sent:
         c.wait_send()
 
     @pl.when(high_edge)
     def _():
-        for c in up + onward_far:
+        for c in up + onward_far + [across]:
             c.wait_send()
 
     @pl.when(jnp.logical_not(high_edge))
@@ -382,26 +497,54 @@
     @pl.when(low_edge)
     def _():
         down.wait_send()
+        upward.wait_send()
         backward_far.wait_send()
 
     @pl.when(jnp.logical_not(low_edge))
     def _():
         backward.wait_send()
 
-
-def wave_part(zr, zone_count, eta, phi, vol, lft, spd):
-    vmem = pl.BlockSpec(memory_space=pltpu.VMEM)
+    for u in range(8):
+        for c in put_out(u):
+            c.wait()
+
+
+def pass_on(a, b, a_out, b_out, held, sem, sem_out):
+    pairs = [(k, i) for i in range(8) for k in range(2)]
+    loads = [pltpu.make_async_copy((a, b)[k].at[i], held.at[k, i], sem.at[k, i]) for k, i in pairs]
+    stores = [pltpu.make_async_copy(held.at[k, i], (a_out, b_out)[k].at[i], sem_out.at[k, i]) for k, i in pairs]
+    for c in loads:
+        c.start()
+    for load, store in zip(loads, stores):
+        load.wait()
+        store.start()
+    for c in stores:
+        c.wait()
+
+
+def on_device(eta_hat, phi_hat, zone_rows, zone_count, volume, lift, stream_speed, surface_blocks):
+    smem = pl.BlockSpec(memory_space=pltpu.SMEM)
     anyw = pl.BlockSpec(memory_space=pl.ANY)
-    return pl.pallas_call(
+    field = jax.ShapeDtypeStruct((8, 48, 1024), F32)
+    results = pl.pallas_call(
         wave_kernel,
-        out_shape=(
-            jax.ShapeDtypeStruct((10, 4, EXT), F32),
-            jax.ShapeDtypeStruct((4, 48, 1024), F32),
-            jax.ShapeDtypeStruct((4, 8, 48, 128), F32),
-        ),
-        in_specs=[anyw, pl.BlockSpec(memory_space=pltpu.SMEM), anyw, anyw, anyw, anyw, anyw],
-        out_specs=(vmem, anyw, anyw),
+        out_shape=(field, field),
+        in_specs=[anyw, smem, smem, anyw, anyw, anyw, anyw, anyw],
+        out_specs=(anyw, anyw),
         scratch_shapes=[
+            pltpu.VMEM((10, 4, EXT), F32),
+            pltpu.VMEM((4, 48, 1024), F32),
+            pltpu.VMEM((2, 48, 128), F32),
+            pltpu.VMEM((2, 48, 128), F32),
+            pltpu.VMEM((2, 2, 8, 48, 128), F32),
+            pltpu.VMEM((8, 48, 1024), F32),
+            pltpu.VMEM((8, 48, 1024), F32),
+            pltpu.VMEM((8, 48, 1024), F32),
+            pltpu.VMEM((8, 48, 1024), F32),
+            pltpu.VMEM((10, 48, 1024), F32),
+            pltpu.VMEM((9, 48, 1024), F32),
+            pltpu.VMEM((8, 48, 1024), F32),
+            pltpu.VMEM((8, 48, 1024), F32),
             pltpu.VMEM((2, 2, 4, 64, 512), F32),
             pltpu.VMEM((2, 4, 4, 2, 8, 256), F32),
             pltpu.VMEM((2, 4, 4, 3, 8, 512), F32),
@@ -423,123 +566,23 @@
             pltpu.VMEM((64, 1024), F32),
             pltpu.SemaphoreType.DMA((N_SEM,)),
             pltpu.SemaphoreType.DMA((N_SEM,)),
-            pltpu.SemaphoreType.DMA((4,)),
+            pltpu.SemaphoreType.DMA((11,)),
+            pltpu.SemaphoreType.DMA((2, 8)),
         ],
         compiler_params=pltpu.CompilerParams(
             collective_id=0, has_side_effects=True, vmem_limit_bytes=60 * 1024 * 1024
         ),
         name="wave_part",
-    )(zr, zone_count, eta, phi, vol, lft, spd)
-
-
-def field_kernel(marks, hr, planes, cols, vol, lft, spd, vol_out, lft_out, rv, rl, fx):
-    t = pl.program_id(0)
-    s = lax.axis_index("stream")
-    g = lax.axis_index("girth")
-    level8 = iota((48, 128), 0).astype(F32) - 23.5
-    rise_z = jnp.exp(level8 * 0.0625)
-    lane = iota((48, 128), 1)
-    row = iota((48, 128), 0)
-
-    def surface(plane, i):
-        cs = slice(128 * i, 128 * (i + 1))
-        return [hr[plane, k : k + 1, cs] for k in range(4)]
-
-    def relax_v(v, here):
-        goal = jnp.clip(here[0] - level8, 0.0, 1.0)
-        return here[3] * goal + (1.0 - here[3]) * v
-
-    def relax_l(l, here):
-        return here[2] * jnp.minimum(rise_z * here[1], 1.0) + (1.0 - here[3]) * l
-
-    def group(i):
-        return slice(128 * i, 128 * (i + 1))
-
-    now = lax.rem(t, 3)
-    one = lax.rem(t + 2, 3)
-    two = lax.rem(t + 1, 3)
-
-    @pl.when(t < 8)
-    def _():
-        for i in range(8):
-            here = surface(t, i + 1)
-            v = relax_v(vol[0, :, group(i)], here)
-            rv[now, :, group(i)] = v
-            fx[now, :, group(i)] = spd[0, :, group(i)] * v
-            rl[now, :, group(i)] = relax_l(lft[0, :, group(i)], here)
-
-    @pl.when(t == 0)
-    def _():
-        for i in range(8):
-            here = surface(8, i + 1)
-            v = relax_v(planes[0, :, group(i)], here)
-            l = relax_l(planes[2, :, group(i)], here)
-            fx[2, :, group(i)] = jnp.where(s > 0, planes[1, :, group(i)] * v, 0.0)
-            rl[2, :, group(i)] = jnp.where(s > 0, l, 0.0)
-
-    @pl.when(t == 8)
-    def _():
-        for i in range(8):
-            l = relax_l(planes[3, :, group(i)], surface(9, i + 1))
-            rl[2, :, group(i)] = jnp.where(s < 63, l, 0.0)
-
-    @pl.when(t >= 1)
-    def _():
-        u = t - 1
-        mark2 = jnp.concatenate(
-            [jnp.full((8, 128), 2.0 * marks[u, k].astype(F32), F32) for k in range(6)], axis=0
-        )
-        here = surface(u, 0)
-        v_left = jnp.where(g > 0, relax_v(cols[0, u], here), 0.0)
-        l_left = jnp.where(g > 0, relax_l(cols[1, u], here), 0.0)
-        here = surface(u, 9)
-        v_right = jnp.where(g < 3, relax_v(cols[2, u], here), 0.0)
-        l_right = jnp.where(g < 3, relax_l(cols[3, u], here), 0.0)
-        v = rv[one, :, group(0)]
-        l = rl[one, :, group(0)]
-        v_fore, l_fore = pltpu.roll(v_left, 1, 1), pltpu.roll(l_left, 1, 1)
-        v_back, l_back = pltpu.roll(v, 127, 1), pltpu.roll(l, 127, 1)
-        for i in range(8):
-            if i < 7:
-                v_then, l_then = rv[one, :, group(i + 1)], rl[one, :, group(i + 1)]
-            else:
-                v_then, l_then = v_right, l_right
-            v_fore_own, l_fore_own = pltpu.roll(v, 1, 1), pltpu.roll(l, 1, 1)
-            v_back_then, l_back_then = pltpu.roll(v_then, 127, 1), pltpu.roll(l_then, 127, 1)
-            v_y = jnp.where(lane == 0, v_fore, v_fore_own) + jnp.where(lane == 127, v_back_then, v_back)
-            l_y = jnp.where(lane == 0, l_fore, l_fore_own) + jnp.where(lane == 127, l_back_then, l_back)
-            face = jnp.maximum(l, 0.0) * v + jnp.minimum(l, 0.0) * pltpu.roll(v, 47, 0)
-            face = jnp.where(row == 47, 0.0, face)
-            div = face - pltpu.roll(face, 1, 0)
-            upwind = fx[one, :, group(i)] - fx[two, :, group(i)]
-            sharpen = mark2 * (v * (1.0 - v) * (2.0 * v - 1.0))
-            vol_out[0, :, group(i)] = v - 0.3 * (upwind + div) + 0.1 * (v_y - 2.0 * v) + sharpen
-            l_z = jnp.where(row == 47, 0.0, pltpu.roll(l, 47, 0)) + jnp.where(row == 0, 0.0, pltpu.roll(l, 1, 0))
-            l_x = rl[now, :, group(i)] + rl[two, :, group(i)]
-            lft_out[0, :, group(i)] = l + 0.15 * (l_x + l_y + l_z - 6.0 * l)
-            v, l = v_then, l_then
-            v_fore, l_fore, v_back, l_back = v_fore_own, l_fore_own, v_back_then, l_back_then
-
-
-def field_part(marks, hr, planes, cols, vol, lft, spd):
-    vmem = pl.BlockSpec(memory_space=pltpu.VMEM)
-    plane = pl.BlockSpec((1, 48, 1024), lambda t: (jnp.minimum(t, 7), 0, 0))
-    out = pl.BlockSpec((1, 48, 1024), lambda t: (jnp.maximum(t - 1, 0), 0, 0))
+    )(zone_rows.T, zone_count, surface_blocks, eta_hat, phi_hat, volume, lift, stream_speed)
     return pl.pallas_call(
-        field_kernel,
-        grid=(9,),
-        out_shape=(jax.ShapeDtypeStruct((8, 48, 1024), F32),) * 2,
-        in_specs=[pl.BlockSpec(memory_space=pltpu.SMEM), vmem, vmem, vmem, plane, plane, plane],
-        out_specs=(out, out),
-        scratch_shapes=[pltpu.VMEM((3, 48, 1024), F32)] * 3,
+        pass_on,
+        out_shape=(field, field),
+        in_specs=[anyw, anyw],
+        out_specs=(anyw, anyw),
+        scratch_shapes=[pltpu.VMEM((2, 8, 48, 1024), F32), pltpu.SemaphoreType.DMA((2, 8)), pltpu.SemaphoreType.DMA((2, 8))],
         compiler_params=pltpu.CompilerParams(vmem_limit_bytes=60 * 1024 * 1024),
-        name="field_part",
-    )(marks, hr, planes, cols, vol, lft, spd)
-
-
-def on_device(eta_hat, phi_hat, zone_rows, zone_count, volume, lift, stream_speed, surface_blocks):
-    hr, planes, cols = wave_part(zone_rows.T, zone_count, eta_hat, phi_hat, volume, lift, stream_speed)
-    return field_part(surface_blocks, hr, planes, cols, volume, lift, stream_speed)
+        name="pass_on",
+    )(*results)
 
 
 def solution(mesh):

time: 77.1 us -> 63.5 us (0.82)
  Pallas kernels: 75.6 us -> 62.1 us
    pallas_call x2, Pallas kernels: 75.6 us -> 62.1 us  [the longest x1 58.9 us: on_device(): pl.pallas_call(wave_kernel, out_shape=(field, field), in_specs=[anyw, sme...]
where the time goes in v3:
time: 63.5 us; the launch traced here: 63.4 us
  Pallas kernels  62.1 us (98%)
  between operations  1.29 us (2%)
    pallas_call x1, Pallas kernels, on_device(): pl.pallas_call(wave_kernel, out_shape=(field, field), in_specs=[anyw, sme...  58.9 us
    pallas_call x1, Pallas kernels, on_device(): pl.pallas_call(pass_on, out_shape=(field, field), in_specs=[anyw, anyw],...  3.17 us

profile of v3, /device:TPU:33, one launch (start us, length us, event | category | flops | bytes accessed | tf_op | source)
XLA Modules:
  0.0 63.4 jit_solution(11341100884266702470)
XLA Ops:
  1.3 58.9 %wave_part.1 = (f32[8,48,1024]{2,1,0:T(8,128)}, f32[8,48,1024]{2,1,0:T(8,128)}) custom-call(s32[8,64]{1,0:T(8,128)} %bitcast.1, s32[1]{0:T(128)S(6)} %copy.10.zc_ref, s32[8,6]{1,0:T(8,128)} %marks.1, f32[64,1024]{1,0:T(8,128)} %eta.1, f32[64,1024]{1,0:T(8,128)} %phi_hbm.1, f32[8,48,1024]{2,1,0:T(8,128)} %vol.1, f32[8,48,1024]{2,1,0:T(8,128)} %lft.1, ...), custom_call_target="tpu_custom_call" | custom-call | tf_op jit(solution)/shard_map/wave_part/pallas_call | solution.py:529
  60.2 3.2 %pass_on.1 = (f32[8,48,1024]{2,1,0:T(8,128)}, f32[8,48,1024]{2,1,0:T(8,128)}) custom-call(f32[8,48,1024]{2,1,0:T(8,128)} %get-tuple-element.4.a, f32[8,48,1024]{2,1,0:T(8,128)} %get-tuple-element.5.b), custom_call_target="tpu_custom_call" | custom-call | tf_op jit(solution)/shard_map/pass_on/pallas_call | solution.py:577

commit v4 on v3

--- a/solution.py
+++ b/solution.py
@@ -12,8 +12,8 @@
 MESH = pl.DeviceIdType.MESH
 EXT = 1280
 
-AG, RS, RZ, GA, ROWS, COLS, PLANES, RELAY = 0, 12, 24, 30, 33, 35, 37, 41
-N_SEM = 46
+AG, RS, RZ, GA, ROWS, COLS, PLANES, RELAY = 0, 12, 24, 30, 33, 35, 37, 42
+N_SEM = 47
 
 
 def iota(shape, dim):
@@ -112,7 +112,7 @@
         pltpu.make_async_copy(lft, lv, lsem.at[9]),
         pltpu.make_async_copy(spd, sv, lsem.at[10]),
     ]
-    for c in fetched + fields:
+    for c in fetched:
         c.start()
 
     s_next = lax.rem(s + 1, 64)
@@ -154,10 +154,16 @@
     high_edge = jnp.logical_and(x == 3, y == 3)
     low_edge = jnp.logical_and(x == 0, y == 0)
 
-    up = [copy(f.at[7], relay.at[k], RELAY + k, on_z(1)) for k, f in enumerate((vol, spd))]
-    across = copy(lft.at[7], relay.at[2], RELAY + 2, at(zh, 0, 0))
-    upward = copy(relay.at[2], planes.at[2], PLANES + 2, on_z(1))
-    down = copy(lft.at[0], relay.at[0], RELAY + 3, on_z(-1))
+    def piece(ref, k):
+        return ref.at[k] if k < 2 else ref.at[2, pl.ds(0, 24) if k == 3 else pl.ds(24, 24)]
+
+    def own(k):
+        return (vol.at[7], spd.at[7], lft.at[7, pl.ds(24, 24)], lft.at[7, pl.ds(0, 24)])[k]
+
+    up = [copy(own(k), piece(relay, k), RELAY + k, on_z(1)) for k in (0, 1, 3)]
+    across = copy(own(2), piece(relay, 2), RELAY + 2, at(zh, 0, 0))
+    upward = copy(piece(relay, 2), piece(planes, 2), PLANES + 2, on_z(1))
+    down = copy(lft.at[0], relay.at[0], RELAY + 4, on_z(-1))
 
     @pl.when(high_edge)
     def _():
@@ -212,20 +218,6 @@
         gat[q, 3].wait_recv()
         gat[q, 5] = start(ag.at[q, 1, 2], ag.at[q, 1, 3], AG + 6 * q + 5, first[q](-1))
 
-    for c in fields[:4]:
-        c.wait()
-    lane = iota((48, 128), 1)
-    for side, at_lane in ((0, 127), (1, 0)):
-        packed = jnp.zeros((48, 128), F32)
-        for f in range(2):
-            for p in range(8):
-                packed = jnp.where(lane == 8 * f + p, ecol[side, f, p, :, at_lane : at_lane + 1], packed)
-        cmsg[side] = packed
-    raw = [
-        start(cmsg.at[0], cin.at[0], COLS, (s, girth(1))),
-        start(cmsg.at[1], cin.at[1], COLS + 1, (s, girth(3))),
-    ]
-
     def fill_e(i, _):
         row = pl.multiple_of(i * 32, 32)
         a = (row + iota((32, 1), 0)).astype(F32)
@@ -275,10 +267,26 @@
         ps[q, 2, 2:4] = ps[q, 2, 2:4] + ob[q, 1]
         near[q, 5] = start(ps.at[q, 2, pl.ds(2, 2)], nb.at[q, 1, pl.ds(2, 2)], b + 5, left)
 
-    onward = [copy(f.at[7], planes.at[k], PLANES + k, (s_next, g)) for k, f in enumerate((vol, spd, lft))]
-    onward_far = [copy(relay.at[k], planes.at[k], PLANES + k, at(zh, 0, 0)) for k in range(2)]
-    backward = copy(lft.at[0], planes.at[3], PLANES + 3, (s_prev, g))
-    backward_far = copy(relay.at[0], planes.at[3], PLANES + 3, at(zh, 3, 3))
+    for c in fields:
+        c.start()
+    for c in fields[:4]:
+        c.wait()
+    lane = iota((48, 128), 1)
+    for side, at_lane in ((0, 127), (1, 0)):
+        packed = jnp.zeros((48, 128), F32)
+        for f in range(2):
+            for p in range(8):
+                packed = jnp.where(lane == 8 * f + p, ecol[side, f, p, :, at_lane : at_lane + 1], packed)
+        cmsg[side] = packed
+    raw = [
+        start(cmsg.at[0], cin.at[0], COLS, (s, girth(1))),
+        start(cmsg.at[1], cin.at[1], COLS + 1, (s, girth(3))),
+    ]
+
+    onward = [copy(own(k), piece(planes, k), PLANES + k, (s_next, g)) for k in range(4)]
+    onward_far = [copy(piece(relay, k), piece(planes, k), PLANES + k, at(zh, 0, 0)) for k in (0, 1, 3)]
+    backward = copy(lft.at[0], planes.at[3], PLANES + 4, (s_prev, g))
+    backward_far = copy(relay.at[0], planes.at[3], PLANES + 4, at(zh, 3, 3))
 
     @pl.when(high_edge)
     def _():
@@ -317,16 +325,14 @@
 
     @pl.when(high_edge)
     def _():
-        for k in range(2):
-            up[k].wait_recv()
-            onward_far[k].start()
+        for c, d in zip(up, onward_far):
+            c.wait_recv()
+            d.start()
 
     @pl.when(low_edge)
     def _():
         down.wait_recv()
         backward_far.start()
-        across.wait_recv()
-        upward.start()
 
     hi, lo = split(xp[...].reshape(24, 1024))
     moved = dot(hi, perm[...]) + dot(lo, perm[...])
@@ -337,6 +343,11 @@
         last.append(start(xg.at[g], xg.at[g], GA + j - 1, (s, girth(j))))
     for c in last:
         c.wait_recv()
+
+    @pl.when(low_edge)
+    def _():
+        across.wait_recv()
+        upward.start()
 
     for gg in range(4):
         os = slice(128 * gg, 128 * (gg + 1))

time: 63.5 us -> 61.3 us (0.965)
  Pallas kernels: 62.1 us -> 59.9 us
    pallas_call x1, Pallas kernels: 58.9 us -> 56.7 us  [on_device(): pl.pallas_call(wave_kernel, out_shape=(field, field), in_specs=[anyw, sme...]
where the time goes in v4:
time: 61.3 us; the launch traced here: 61.2 us
  Pallas kernels  59.9 us (98%)
  between operations  1.29 us (2%)
    pallas_call x1, Pallas kernels, on_device(): pl.pallas_call(wave_kernel, out_shape=(field, field), in_specs=[anyw, sme...  56.7 us
    pallas_call x1, Pallas kernels, on_device(): pl.pallas_call(pass_on, out_shape=(field, field), in_specs=[anyw, anyw],...  3.17 us

profile of v4, /device:TPU:33, one launch (start us, length us, event | category | flops | bytes accessed | tf_op | source)
XLA Modules:
  0.0 61.2 jit_solution(11832494302519238418)
XLA Ops:
  1.3 56.7 %wave_part.1 = (f32[8,48,1024]{2,1,0:T(8,128)}, f32[8,48,1024]{2,1,0:T(8,128)}) custom-call(s32[8,64]{1,0:T(8,128)} %bitcast.1, s32[1]{0:T(128)S(6)} %copy.10.zc_ref, s32[8,6]{1,0:T(8,128)} %marks.1, f32[64,1024]{1,0:T(8,128)} %eta.1, f32[64,1024]{1,0:T(8,128)} %phi_hbm.1, f32[8,48,1024]{2,1,0:T(8,128)} %vol.1, f32[8,48,1024]{2,1,0:T(8,128)} %lft.1, ...), custom_call_target="tpu_custom_call" | custom-call | tf_op jit(solution)/shard_map/wave_part/pallas_call | solution.py:540
  58.0 3.2 %pass_on.1 = (f32[8,48,1024]{2,1,0:T(8,128)}, f32[8,48,1024]{2,1,0:T(8,128)}) custom-call(f32[8,48,1024]{2,1,0:T(8,128)} %get-tuple-element.4.a, f32[8,48,1024]{2,1,0:T(8,128)} %get-tuple-element.5.b), custom_call_target="tpu_custom_call" | custom-call | tf_op jit(solution)/shard_map/pass_on/pallas_call | solution.py:588

commit v5 on v4

--- a/solution.py
+++ b/solution.py
@@ -60,7 +60,7 @@
 
 def dot3(left, right):
     (lh, ll), (rh, rl) = left, right
-    return dot(lh, rh) + (dot(lh, rl) + dot(ll, rh))
+    return dot(jnp.concatenate([lh, ll, lh], axis=1), jnp.concatenate([rh, rh, rl], axis=0))
 
 
 def pick(index, values):
@@ -153,6 +153,8 @@
         gat[q, 1] = start(ag.at[q, 0, 0], ag.at[q, 0, 2], AG + 6 * q + 1, first[q](-1))
     high_edge = jnp.logical_and(x == 3, y == 3)
     low_edge = jnp.logical_and(x == 0, y == 0)
+    high_out, high_in = jnp.logical_and(high_edge, zh < 3), jnp.logical_and(high_edge, zh > 0)
+    low_out, low_in = jnp.logical_and(low_edge, zh > 0), jnp.logical_and(low_edge, zh < 3)
 
     def piece(ref, k):
         return ref.at[k] if k < 2 else ref.at[2, pl.ds(0, 24) if k == 3 else pl.ds(24, 24)]
@@ -165,12 +167,12 @@
     upward = copy(piece(relay, 2), piece(planes, 2), PLANES + 2, on_z(1))
     down = copy(lft.at[0], relay.at[0], RELAY + 4, on_z(-1))
 
-    @pl.when(high_edge)
+    @pl.when(high_out)
     def _():
         for c in up:
             c.start()
 
-    @pl.when(low_edge)
+    @pl.when(low_out)
     def _():
         down.start()
 
@@ -288,7 +290,7 @@
     backward = copy(lft.at[0], planes.at[3], PLANES + 4, (s_prev, g))
     backward_far = copy(relay.at[0], planes.at[3], PLANES + 4, at(zh, 3, 3))
 
-    @pl.when(high_edge)
+    @pl.when(high_out)
     def _():
         across.start()
 
@@ -323,28 +325,30 @@
         mid[q, 2].wait_recv()
         xp[:, :, q * 512 : (q + 1) * 512] = zs[q, 0] + zn[q, 0] + zn[q, 1]
 
-    @pl.when(high_edge)
+    @pl.when(high_in)
     def _():
         for c, d in zip(up, onward_far):
             c.wait_recv()
             d.start()
 
-    @pl.when(low_edge)
+    @pl.when(low_in)
     def _():
         down.wait_recv()
         backward_far.start()
 
     hi, lo = split(xp[...].reshape(24, 1024))
-    moved = dot(hi, perm[...]) + dot(lo, perm[...])
-    moved = moved.reshape(3, 8, 1024)
+    moved = dot(jnp.concatenate([hi, lo], axis=0), perm[...])
+    moved = (moved[:24] + moved[24:]).reshape(3, 8, 1024)
     xg[g] = moved
-    last = []
-    for j in (1, 2, 3):
-        last.append(start(xg.at[g], xg.at[g], GA + j - 1, (s, girth(j))))
+    beside, over = g + 1 - 2 * lax.rem(g, 2), girth(2)
+    far = start(xg.at[g], xg.at[g], GA, (s, over))
+    last = [start(xg.at[g], xg.at[g], GA + 1, (s, beside))]
+    far.wait_recv()
+    last.append(start(xg.at[over], xg.at[over], GA + 2, (s, beside)))
     for c in last:
         c.wait_recv()
 
-    @pl.when(low_edge)
+    @pl.when(low_in)
     def _():
         across.wait_recv()
         upward.start()
@@ -393,10 +397,17 @@
             for k in range(4):
                 hr[p, k : k + 1, cs] = parts[k][p : p + 1]
 
-    rows = [
-        start(hr.at[7], hr.at[8], ROWS, (s_next, g)),
-        start(hr.at[0], hr.at[9], ROWS + 1, (s_prev, g)),
-    ]
+    row_next = copy(hr.at[7], hr.at[8], ROWS, (s_next, g))
+    row_prev = copy(hr.at[0], hr.at[9], ROWS + 1, (s_prev, g))
+
+    @pl.when(s < 63)
+    def _():
+        row_next.start()
+
+    @pl.when(s > 0)
+    def _():
+        row_prev.start()
+
 
     for c in fields[4:]:
         c.wait()
@@ -480,8 +491,17 @@
         return 0
 
     lax.fori_loop(0, 6, step, 0)
-    for c in rows + onward + [backward]:
-        c.wait_recv()
+
+    @pl.when(s > 0)
+    def _():
+        for c in [row_next] + onward:
+            c.wait_recv()
+
+    @pl.when(s < 63)
+    def _():
+        row_prev.wait_recv()
+        backward.wait_recv()
+
     for i in range(8):
         here = surface(8, i + 1)
         v = relax_v(planes[0, :, group(i)], here)
@@ -495,9 +515,22 @@
     for c in sent:
         c.wait_send()
 
-    @pl.when(high_edge)
-    def _():
-        for c in up + onward_far + [across]:
+    @pl.when(s < 63)
+    def _():
+        row_next.wait_send()
+
+    @pl.when(s > 0)
+    def _():
+        row_prev.wait_send()
+
+    @pl.when(high_out)
+    def _():
+        for c in up + [across]:
+            c.wait_send()
+
+    @pl.when(high_in)
+    def _():
+        for c in onward_far:
             c.wait_send()
 
     @pl.when(jnp.logical_not(high_edge))
@@ -505,11 +538,14 @@
         for c in onward:
             c.wait_send()
 
-    @pl.when(low_edge)
+    @pl.when(low_out)
     def _():
         down.wait_send()
+
+    @pl.when(low_in)
+    def _():
+        backward_far.wait_send()
         upward.wait_send()
-        backward_far.wait_send()
 
     @pl.when(jnp.logical_not(low_edge))
     def _():

time: 61.3 us -> 60.8 us (level)
  the two profiles are of different devices: /device:TPU:33 before, /device:TPU:64 now
where the time goes in v5:
time: 60.8 us; the launch traced here: 60.7 us
  Pallas kernels  59.4 us (98%)
  between operations  1.29 us (2%)
    pallas_call x1, Pallas kernels, on_device(): pl.pallas_call(wave_kernel, out_shape=(field, field), in_specs=[anyw, sme...  56.2 us
    pallas_call x1, Pallas kernels, on_device(): pl.pallas_call(pass_on, out_shape=(field, field), in_specs=[anyw, anyw],...  3.17 us

profile of v5, /device:TPU:64, one launch (start us, length us, event | category | flops | bytes accessed | tf_op | source)
XLA Modules:
  0.0 60.7 jit_solution(8594501278737444305)
XLA Ops:
  1.3 56.2 %wave_part.1 = (f32[8,48,1024]{2,1,0:T(8,128)}, f32[8,48,1024]{2,1,0:T(8,128)}) custom-call(s32[8,64]{1,0:T(8,128)} %bitcast.1, s32[1]{0:T(128)S(6)} %copy.10.zc_ref, s32[8,6]{1,0:T(8,128)} %marks.1, f32[64,1024]{1,0:T(8,128)} %eta.1, f32[64,1024]{1,0:T(8,128)} %phi_hbm.1, f32[8,48,1024]{2,1,0:T(8,128)} %vol.1, f32[8,48,1024]{2,1,0:T(8,128)} %lft.1, ...), custom_call_target="tpu_custom_call" | custom-call | tf_op jit(solution)/shard_map/wave_part/pallas_call | solution.py:576
  57.5 3.2 %pass_on.1 = (f32[8,48,1024]{2,1,0:T(8,128)}, f32[8,48,1024]{2,1,0:T(8,128)}) custom-call(f32[8,48,1024]{2,1,0:T(8,128)} %get-tuple-element.4.a, f32[8,48,1024]{2,1,0:T(8,128)} %get-tuple-element.5.b), custom_call_target="tpu_custom_call" | custom-call | tf_op jit(solution)/shard_map/pass_on/pallas_call | solution.py:624

commit v6 on v5

--- a/solution.py
+++ b/solution.py
@@ -557,9 +557,9 @@
 
 
 def pass_on(a, b, a_out, b_out, held, sem, sem_out):
-    pairs = [(k, i) for i in range(8) for k in range(2)]
-    loads = [pltpu.make_async_copy((a, b)[k].at[i], held.at[k, i], sem.at[k, i]) for k, i in pairs]
-    stores = [pltpu.make_async_copy(held.at[k, i], (a_out, b_out)[k].at[i], sem_out.at[k, i]) for k, i in pairs]
+    pairs = [(k, pl.ds(2 * i, 2)) for i in range(4) for k in range(2)]
+    loads = [pltpu.make_async_copy((a, b)[k].at[i], held.at[k, i], sem.at[k, n // 2]) for n, (k, i) in enumerate(pairs)]
+    stores = [pltpu.make_async_copy(held.at[k, i], (a_out, b_out)[k].at[i], sem_out.at[k, n // 2]) for n, (k, i) in enumerate(pairs)]
     for c in loads:
         c.start()
     for load, store in zip(loads, stores):

time: 60.8 us -> 60.6 us (level)
  no operation moved by 1% of the time
where the time goes in v6:
time: 60.6 us; the launch traced here: 60.5 us
  Pallas kernels  59.2 us (98%)
  between operations  1.29 us (2%)
    pallas_call x1, Pallas kernels, on_device(): pl.pallas_call(wave_kernel, out_shape=(field, field), in_specs=[anyw, sme...  56.2 us
    pallas_call x1, Pallas kernels, on_device(): pl.pallas_call(pass_on, out_shape=(field, field), in_specs=[anyw, anyw],...  2.93 us

profile of v6, /device:TPU:64, one launch (start us, length us, event | category | flops | bytes accessed | tf_op | source)
XLA Modules:
  0.0 60.5 jit_solution(7836275763795990874)
XLA Ops:
  1.3 56.2 %wave_part.1 = (f32[8,48,1024]{2,1,0:T(8,128)}, f32[8,48,1024]{2,1,0:T(8,128)}) custom-call(s32[8,64]{1,0:T(8,128)} %bitcast.1, s32[1]{0:T(128)S(6)} %copy.10.zc_ref, s32[8,6]{1,0:T(8,128)} %marks.1, f32[64,1024]{1,0:T(8,128)} %eta.1, f32[64,1024]{1,0:T(8,128)} %phi_hbm.1, f32[8,48,1024]{2,1,0:T(8,128)} %vol.1, f32[8,48,1024]{2,1,0:T(8,128)} %lft.1, ...), custom_call_target="tpu_custom_call" | custom-call | tf_op jit(solution)/shard_map/wave_part/pallas_call | solution.py:576
  57.5 2.9 %pass_on.1 = (f32[8,48,1024]{2,1,0:T(8,128)}, f32[8,48,1024]{2,1,0:T(8,128)}) custom-call(f32[8,48,1024]{2,1,0:T(8,128)} %get-tuple-element.4.a, f32[8,48,1024]{2,1,0:T(8,128)} %get-tuple-element.5.b), custom_call_target="tpu_custom_call" | custom-call | tf_op jit(solution)/shard_map/pass_on/pallas_call | solution.py:624
